TPU v7x, 32 devices: a whole 2x2x4 slice. The times are simulated.
32 devices in a mesh: batch: 8 (over y, x, core), blk: 4 (over z).
Axes of the slice: x: 2, y: 2, z: 4, core: 2. Of those that a mesh axis runs over, the one named last changes fastest.
Arguments:
- tokens: bfloat16 [8, 2048, 1024], P('batch', 'blk'), may hold values from -6 to 6
- lengths: int32 [8, 4], P('batch'), may hold values from 1 to 2045, as said below
- first_gain: float32 [1024], replicated, may hold values from 0.5 to 1.5
- first_shift: float32 [1024], replicated, may hold values from -4 to 4
- second_gain: float32 [1024], replicated, may hold values from 0.5 to 1.5
- second_shift: float32 [1024], replicated, may hold values from -4 to 4
- joint_weight: bfloat16 [1024, 3072], replicated, may hold values from -0.1875 to 0.1875
- joint_bias: float32 [3072], replicated, may hold values from -6 to 6
- dense_weight: bfloat16 [1024, 1024], replicated, may hold values from -1.5 to 1.5
- dense_bias: float32 [1024], replicated, may hold values from -6 to 6
- expand_weight: bfloat16 [1024, 4096], replicated, may hold values from -0.1875 to 0.1875
- expand_bias: float32 [4096], replicated, may hold values from -6 to 6
- reduce_weight: bfloat16 [4096, 1024], replicated, may hold values from -0.09375 to 0.09375
- reduce_bias: float32 [1024], replicated, may hold values from -6 to 6
- cotangent: bfloat16 [8, 2048, 1024], P('batch', 'blk'), may hold values from -6 to 6
Outputs:
- result: bfloat16 [8, 2048, 1024], P('batch', 'blk')
- tokens_gradient: bfloat16 [8, 2048, 1024], P('batch', 'blk')
- first_gain_gradient: float32 [1024], P(('batch', 'blk'))
- first_shift_gradient: float32 [1024], P(('batch', 'blk'))
- second_gain_gradient: float32 [1024], P(('batch', 'blk'))
- second_shift_gradient: float32 [1024], P(('batch', 'blk'))
- joint_weight_gradient: float32 [1024, 3072], P(('batch', 'blk'))
- joint_bias_gradient: float32 [2048], P(('batch', 'blk'))
- value_bias_gradient: float32 [1024], P(('batch', 'blk'))
- dense_weight_gradient: float32 [1024, 1024], P(('batch', 'blk'))
- dense_bias_gradient: float32 [1024], P(('batch', 'blk'))
- expand_weight_gradient: float32 [1024, 4096], P(('batch', 'blk'))
- expand_bias_gradient: float32 [4096], P(('batch', 'blk'))
- reduce_weight_gradient: float32 [4096, 1024], P(('batch', 'blk'))
- reduce_bias_gradient: float32 [1024], P(('batch', 'blk'))
Inputs may be any that keep to these rules, and one draw needn't show every extreme that they name: `lengths`: each row sums to 2048. In every group of 1 row that one index of batch holds, one row drawn from the seed has one document of 2045 tokens and 3 documents of one token, a number of them drawn from the seed before it and the others after it.
All inputs are finite; a program needn't handle non-finite values.
Results may differ from a plain program's by a relative error of at most 0.017.
Values may be sent and summed in bfloat16 or wider, within the bound.
No kernel may reach another device: no remote copies, remote signals or barrier semaphores. Data moves between devices by JAX's collectives and lax.ppermute only.
A program may use at most 320 MiB of HBM per device.

v0:
```python
from functools import partial

import jax
import jax.numpy as jnp
from jax import lax
from jax.sharding import PartitionSpec as P

HEADS = 16
HEAD = 64
ROTARY = 16


EPSILON = 1e-05
MASKED = -1e30


def doc_tables(lengths, positions):
    doc_ends = jnp.cumsum(lengths, axis=-1)
    doc_starts = doc_ends - lengths
    doc_number = jnp.sum(
        (positions[None, :, None] >= doc_ends[:, None, :]).astype(jnp.int32), axis=-1
    )
    matches = (
        doc_number[:, :, None] == jnp.arange(lengths.shape[-1], dtype=jnp.int32)[None, None, :]
    )
    begins = jnp.sum(jnp.where(matches, doc_starts[:, None, :], 0), axis=-1)
    return (doc_number, positions[None, :] - begins)


def angles(offsets):
    half_width = ROTARY // 2
    inverse = 10000.0 ** (-2.0 * jnp.arange(half_width, dtype=jnp.float32) / ROTARY)
    phase = offsets.astype(jnp.float32)[..., None] * inverse
    return (jnp.cos(phase), jnp.sin(phase))


def rotate(values, cosine, sine_table, direction):
    half_width = cosine.shape[-1]
    lead_part = values[..., :half_width]
    tail_part = values[..., half_width : 2 * half_width]
    cosine = cosine[:, :, None, :]
    sine_table = sine_table[:, :, None, :] * direction
    return jnp.concatenate(
        [
            lead_part * cosine - tail_part * sine_table,
            tail_part * cosine + lead_part * sine_table,
            values[..., 2 * half_width :],
        ],
        axis=-1,
    )


def normalize(values, gain_row, shift_row):
    center = values - jnp.mean(values, axis=-1, keepdims=True)
    spread = jnp.mean(center * center, axis=-1, keepdims=True)
    inverse_root = lax.rsqrt(spread + EPSILON)
    unit_rows = center * inverse_root
    return (unit_rows * gain_row + shift_row, unit_rows, inverse_root)


def normalize_back(upstream, unit_rows, inverse_root, gain_row):
    scaled_back = upstream * gain_row
    input_back = inverse_root * (
        scaled_back
        - jnp.mean(scaled_back, axis=-1, keepdims=True)
        - unit_rows * jnp.mean(scaled_back * unit_rows, axis=-1, keepdims=True)
    )
    return (input_back, jnp.sum(upstream * unit_rows, axis=0), jnp.sum(upstream, axis=0))


def outer(left_rows, right_rows):
    return lax.dot_general(
        left_rows, right_rows, (((0,), (0,)), ((), ())), preferred_element_type=jnp.float32
    )


def against(left_rows, weight_rows):
    return lax.dot_general(
        left_rows, weight_rows, (((1,), (1,)), ((), ())), preferred_element_type=jnp.float32
    )


def over_piece(stepper, running, segment, stride):
    sub_count = segment.shape[1] // stride

    def one_turn(position, current):
        part_rows = lax.dynamic_slice_in_dim(segment, position * stride, stride, 1)
        return stepper(current, part_rows, position * stride)

    return lax.fori_loop(0, sub_count, one_turn, running)


def local(
    tokens,
    lengths,
    first_gain,
    first_shift,
    second_gain,
    second_shift,
    joint_weight,
    joint_bias,
    dense_weight,
    dense_bias,
    expand_weight,
    expand_bias,
    reduce_weight,
    reduce_bias,
    cotangent,
):
    sequences, stride, model_width = tokens.shape
    cycle_size = lax.axis_size("blk")
    seq_total = stride * cycle_size
    rank_here = lax.axis_index("blk")
    row_count = sequences * stride
    factor = HEAD ** (-0.5)
    head_shape = (sequences, stride, HEADS, HEAD)
    places = jnp.arange(seq_total, dtype=jnp.int32)
    number_all, offset_all = doc_tables(lengths, places)
    first_place = rank_here * stride
    query_number = lax.dynamic_slice_in_dim(number_all, first_place, stride, 1)
    query_offset = lax.dynamic_slice_in_dim(offset_all, first_place, stride, 1)
    query_place = first_place + jnp.arange(stride, dtype=jnp.int32)
    last_place = first_place + stride - 1
    cosine, sine_table = angles(query_offset)
    inputs = tokens.reshape(row_count, model_width).astype(jnp.float32)
    first_norm, first_unit, first_scale = normalize(inputs, first_gain, first_shift)
    normed = first_norm.astype(jnp.bfloat16)
    joint_out = jnp.dot(normed, joint_weight, preferred_element_type=jnp.float32) + joint_bias
    queries = rotate(
        joint_out[:, :model_width].reshape(head_shape), cosine, sine_table, 1.0
    ).astype(jnp.bfloat16)
    key_rows = rotate(
        joint_out[:, model_width : 2 * model_width].reshape(head_shape), cosine, sine_table, 1.0
    ).astype(jnp.bfloat16)
    value_rows = joint_out[:, 2 * model_width :].astype(jnp.bfloat16)
    pair_local = jnp.concatenate(
        [
            key_rows.reshape(sequences, stride, model_width),
            value_rows.reshape(sequences, stride, model_width),
        ],
        axis=-1,
    )

    def masked_scores(key_part, begin_row, row_span):
        key_number = lax.dynamic_slice_in_dim(number_all, begin_row, row_span, 1)
        key_place = begin_row + jnp.arange(row_span, dtype=jnp.int32)
        allowed = (query_number[:, :, None] == key_number[:, None, :]) & (
            key_place[None, None, :] <= query_place[None, :, None]
        )
        allowed = allowed[:, None]
        scores = (
            jnp.einsum("sqhd,skhd->shqk", queries, key_part, preferred_element_type=jnp.float32)
            * factor
        )
        return (jnp.where(allowed, scores, MASKED), allowed)

    def split_piece(segment):
        row_span = segment.shape[1]
        key_part = segment[:, :, :model_width].reshape(sequences, row_span, HEADS, HEAD)
        value_part = segment[:, :, model_width:].reshape(sequences, row_span, HEADS, HEAD)
        return (key_part, value_part, row_span)

    def gated(kernel):

        def stepper(running, segment, begin_row):
            return lax.cond(
                begin_row <= last_place,
                lambda current: kernel(current, segment, begin_row),
                lambda current: current,
                running,
            )

        return stepper

    def forward_kernel(running, segment, begin_row):
        row_peak, row_total, weighted = running
        key_part, value_part, row_span = split_piece(segment)
        scores, allowed = masked_scores(key_part, begin_row, row_span)
        new_peak = jnp.maximum(row_peak, jnp.max(scores, axis=-1))
        shares = jnp.where(allowed, jnp.exp(scores - new_peak[..., None]), 0.0)
        decay_factor = jnp.exp(row_peak - new_peak)
        row_total = row_total * decay_factor + jnp.sum(shares, axis=-1)
        update = jnp.einsum(
            "shqk,skhd->sqhd",
            shares.astype(jnp.bfloat16),
            value_part,
            preferred_element_type=jnp.float32,
        )
        weighted = weighted * jnp.transpose(decay_factor, (0, 2, 1))[..., None] + update
        return (new_peak, row_total, weighted)

    forward_step = gated(forward_kernel)
    initial = (
        jnp.full((sequences, HEADS, stride), MASKED, jnp.float32),
        jnp.zeros((sequences, HEADS, stride), jnp.float32),
        jnp.zeros(head_shape, jnp.float32),
    )
    forward_state = over_piece(
        forward_step, initial, lax.all_gather(pair_local, "blk", axis=1, tiled=True), stride
    )
    row_peak, row_total, weighted = forward_state
    mixed_full = weighted / jnp.transpose(row_total, (0, 2, 1))[..., None]
    log_total = row_peak + jnp.log(row_total)
    mixed = mixed_full.reshape(row_count, model_width).astype(jnp.bfloat16)
    attention_out = jnp.dot(mixed, dense_weight, preferred_element_type=jnp.float32) + dense_bias
    second_norm, second_unit, second_scale = normalize(inputs, second_gain, second_shift)
    second = second_norm.astype(jnp.bfloat16)
    hidden = jnp.dot(second, expand_weight, preferred_element_type=jnp.float32) + expand_bias
    active_full, gelu_pull = jax.vjp(partial(jax.nn.gelu, approximate=False), hidden)
    active = active_full.astype(jnp.bfloat16)
    feed_out = jnp.dot(active, reduce_weight, preferred_element_type=jnp.float32) + reduce_bias
    result = (
        (inputs + attention_out + feed_out)
        .astype(jnp.bfloat16)
        .reshape(sequences, stride, model_width)
    )
    upstream = cotangent.reshape(row_count, model_width)
    dense_grad = outer(mixed, upstream)
    bias_total = jnp.sum(upstream, axis=0, dtype=jnp.float32)
    reduce_grad = outer(active, upstream)
    hidden_grad = gelu_pull(against(upstream, reduce_weight))[0].astype(jnp.bfloat16)
    expand_grad = outer(second, hidden_grad)
    hidden_total = jnp.sum(hidden_grad, axis=0, dtype=jnp.float32)
    input_two, gain_second, shift_second = normalize_back(
        against(hidden_grad, expand_weight), second_unit, second_scale, second_gain
    )
    mixed_grad = against(upstream, dense_weight).astype(jnp.bfloat16)
    out_heads = mixed_grad.reshape(head_shape)
    delta_rows = jnp.transpose(jnp.sum(out_heads * mixed_full, axis=-1), (0, 2, 1))

    def backward_kernel(running, segment, begin_row):
        key_part, value_part, row_span = split_piece(segment)
        scores, allowed = masked_scores(key_part, begin_row, row_span)
        weights_now = jnp.where(allowed, jnp.exp(scores - log_total[..., None]), 0.0)
        weight_grad = jnp.einsum(
            "sqhd,skhd->shqk", out_heads, value_part, preferred_element_type=jnp.float32
        )
        score_grad = (weights_now * (weight_grad - delta_rows[..., None])).astype(jnp.bfloat16)
        query_grad = (
            running[0]
            + jnp.einsum(
                "shqk,skhd->sqhd", score_grad, key_part, preferred_element_type=jnp.float32
            )
            * factor
        )
        value_grad = jnp.einsum(
            "shqk,sqhd->skhd",
            weights_now.astype(jnp.bfloat16),
            out_heads,
            preferred_element_type=jnp.float32,
        )
        key_grad = (
            jnp.einsum("shqk,sqhd->skhd", score_grad, queries, preferred_element_type=jnp.float32)
            * factor
        )
        fresh_rows = jnp.concatenate(
            [
                key_grad.reshape(sequences, row_span, model_width),
                value_grad.reshape(sequences, row_span, model_width),
            ],
            axis=-1,
        )
        pair_grad = lax.dynamic_update_slice_in_dim(running[1], fresh_rows, begin_row, 1)
        return (query_grad, pair_grad)

    backward_step = gated(backward_kernel)
    back_initial = (
        jnp.zeros(head_shape, jnp.float32),
        jnp.zeros((sequences, seq_total, 2 * model_width), jnp.float32),
    )
    back_state = over_piece(
        backward_step, back_initial, lax.all_gather(pair_local, "blk", axis=1, tiled=True), stride
    )
    query_grad = back_state[0]
    pair_mine = lax.psum_scatter(back_state[1], "blk", scatter_dimension=1, tiled=True)
    query_back = rotate(query_grad, cosine, sine_table, -1.0).reshape(row_count, model_width)
    key_back = rotate(
        pair_mine[:, :, :model_width].reshape(head_shape), cosine, sine_table, -1.0
    ).reshape(row_count, model_width)
    value_back = pair_mine[:, :, model_width:].reshape(row_count, model_width)
    joint_back = jnp.concatenate([query_back, key_back, value_back], axis=-1).astype(jnp.bfloat16)
    joint_grad = outer(normed, joint_back)
    joint_total = jnp.sum(joint_back, axis=0, dtype=jnp.float32)
    front_total = joint_total[: 2 * model_width]
    value_total = joint_total[2 * model_width :]
    input_one, gain_first, shift_first = normalize_back(
        against(joint_back, joint_weight), first_unit, first_scale, first_gain
    )
    input_total = (
        (upstream.astype(jnp.float32) + input_one + input_two)
        .astype(jnp.bfloat16)
        .reshape(sequences, stride, model_width)
    )
    summed = (
        lax.psum_scatter(gain_first, ("batch", "blk"), scatter_dimension=0, tiled=True),
        lax.psum_scatter(shift_first, ("batch", "blk"), scatter_dimension=0, tiled=True),
        lax.psum_scatter(gain_second, ("batch", "blk"), scatter_dimension=0, tiled=True),
        lax.psum_scatter(shift_second, ("batch", "blk"), scatter_dimension=0, tiled=True),
        lax.psum_scatter(joint_grad, ("batch", "blk"), scatter_dimension=0, tiled=True),
        lax.psum_scatter(front_total, ("batch", "blk"), scatter_dimension=0, tiled=True),
        lax.psum_scatter(value_total, ("batch", "blk"), scatter_dimension=0, tiled=True),
        lax.psum_scatter(dense_grad, ("batch", "blk"), scatter_dimension=0, tiled=True),
        lax.psum_scatter(bias_total, ("batch", "blk"), scatter_dimension=0, tiled=True),
        lax.psum_scatter(expand_grad, ("batch", "blk"), scatter_dimension=0, tiled=True),
        lax.psum_scatter(hidden_total, ("batch", "blk"), scatter_dimension=0, tiled=True),
        lax.psum_scatter(reduce_grad, ("batch", "blk"), scatter_dimension=0, tiled=True),
    )
    return (
        result,
        input_total,
        summed[0],
        summed[1],
        summed[2],
        summed[3],
        summed[4],
        summed[5],
        summed[6],
        summed[7],
        summed[8],
        summed[9],
        summed[10],
        summed[11],
        summed[8],
    )


def solution(mesh):
    placed = (
        P("batch", "blk", None),
        P("batch", None),
        P(),
        P(),
        P(),
        P(),
        P(),
        P(),
        P(),
        P(),
        P(),
        P(),
        P(),
        P(),
        P("batch", "blk", None),
    )
    return jax.shard_map(
        local,
        mesh=mesh,
        in_specs=placed,
        out_specs=(
            P("batch", "blk", None),
            P("batch", "blk", None),
            P(("batch", "blk")),
            P(("batch", "blk")),
            P(("batch", "blk")),
            P(("batch", "blk")),
            P(("batch", "blk"), None),
            P(("batch", "blk")),
            P(("batch", "blk")),
            P(("batch", "blk"), None),
            P(("batch", "blk")),
            P(("batch", "blk"), None),
            P(("batch", "blk")),
            P(("batch", "blk"), None),
            P(("batch", "blk")),
        ),
        check_vma=False,
    )
```

profile of v0, /device:TPU:0, one launch (start us, length us, event | category | flops | bytes accessed | tf_op | source)
XLA Modules:
  0.0 1783.1 jit_solution(4122173331294959864)
XLA Ops:
  8.8 1.6 fusion.66
  10.5 6.1 convolution_add_fusion
  17.8 2.3 fusion.93
  20.4 2.9 copy.71
  23.3 2.9 copy.69
  26.2 2.4 slice.148
  33.4 3.1 pad_maximum_fusion.1
  38.4 3.5 convolution_convert_fusion
  41.9 2.3 copy.73
  45.2 143.8 %all-gather.2.cloned.1.call-done = bf16[1,2048,2048]{2,1,0:T(8,128)(2,1)} async-done(((bf16[1,512,2048]{2,1,0:T(8,128)(2,1)}), bf16[1,2048,2048]{2,1,0:T(8,128)(2,1)}) %all-gather.2.cloned.1.call-update) | async-done | bytes 8388624 | tf_op jit(solution)/shard_map/all_gather | solution.py:199
  189.0 12.2 copy.72
  202.8 16.0 while.34
  202.8 15.9 conditional.6
  202.8 1.7 constant_dynamic-slice_fusion.1
  204.8 3.9 fusion.4
  208.7 4.0 fusion.6
  212.7 4.7 bitcast_add_fusion
  218.8 3.3 multiply_reduce_fusion
  223.7 7.9 broadcast_in_dim.64
  231.6 44.0 %while.35 = (s32[]{:T(128)}, f32[1,512,16,64]{1,3,2,0:T(8,128)}, f32[1,2048,2048]{1,2,0:T(8,128)}, s32[]{:T(128)}, bf16[1,2048,2048]{1,2,0:T(8,128)(2,1)}, /*ind...) while((s32[]{:T(128)}, f32[1,512,16,64]{1,3,2,0:T(8,128)}, ...), condition=%wide.region_15.16_spmd.clone, body=%wide.region_12.15_spmd.clone.sunk | while | flops 2738095104 | bytes 129880520 | solution.py:90
  232.0 43.3 %conditional.7 = ((f32[1,512,16,64]{1,3,2,0:T(8,128)}, f32[1,2048,2048]{1,2,0:T(8,128)})) conditional(s32[]{:T(128)} %convert_element_type.258, (f32[1,512,16,64]{1,3,2,0:T(8,128)}, f32[1,2048,2048]{1,2,0:T(8,128)}) %tuple.139, (s32[]{:T(128)}, bf16[1,2048,2048]{1,2,0:T(8,128)(2,1)}, s32[1,512]{1,0:T(1,128)S(1)}, s32[1,2048]{1,0:T(1,128)S(1)}, ...), branch_computations={%region_13.13_spmd, %region_14.14_spmd} | conditional | flops 2738095104 | bytes 129878200 | solution.py:166
  232.3 2.7 constant_dynamic-slice_fusion.5
  235.0 9.3 fusion.29
  244.3 11.7 fusion.23
  256.0 10.0 fusion.18
  266.0 4.0 convolution_multiply_fusion
  272.8 2.5 maximum_dynamic-update-slice_fusion
  275.7 4.9 fusion.74
  280.8 27.7 %multiply_convert_fusion = (bf16[512,4096]{1,0:T(8,128)(2,1)}, f32[512,4096]{1,0:T(8,128)}, f32[512,4096]{1,0:T(8,128)}) fusion(f32[4096]{0:T(1024)S(1)} %copy-done.27, bf16[1024,4096]{1,0:T(8,128)(2,1)} %param.33, bf16[1,512,1024]{2,1,0:T(8,128)(2,1)S(1)} %copy-done.4, f32[1024]{0:T(1024)S(1)} %copy-done.28, f32[1024]{0:T(1024)S(1)} %copy-done.25, ...), kind=kOutput, calls=%fused_computation.55 | convolution fusion | flops 4436525056 | bytes 30437376 | tf_op jit(solution)/shard_map/dot_general | solution.py:208
  308.4 13.3 convert_reduce_fusion
  321.8 1.9 copy-done.35
  323.7 8.4 fusion.84
  332.4 12.8 fusion.72
  345.3 2.4 slice.146
  347.7 383.9 %reduce-scatter.6.cloned.1.call-done = f32[1,512,2048]{1,2,0:T(8,128)} async-done(((f32[1,2048,2048]{1,2,0:T(8,128)}), f32[1,512,2048]{1,2,0:T(8,128)}) %reduce-scatter.6.cloned.1.call-update) | async-done | bytes 4194320 | tf_op jit(solution)/shard_map/reduce_scatter | solution.py:275
  731.6 1.8 slice.112
  735.0 2.5 fusion.71
  738.5 9.6 fusion.88
  748.1 8.4 fusion.95
  756.6 7.1 fusion.94
  763.8 2.4 fusion.69
  767.5 4.9 fusion.64
  772.4 2.3 convert_reduce_fusion.2
  774.7 42.3 %all-reduce.8 = (f32[1024]{0:T(1024)S(1)}, f32[1024]{0:T(1024)S(1)}, f32[1024]{0:T(1024)S(1)}, f32[1024]{0:T(1024)S(1)}, f32[2048]{0:T(1024)S(1)}, /*index=5*/f3...) all-reduce(f32[1024]{0:T(1024)S(1)} %get-tuple-element.751, ...), channel_id=3, replica_groups=mesh['batch'=8,'blk'=4] {'batch','blk'}, use_global_device_ids=true, to_apply=%region_22.23.clone | all-reduce | flops 12288 | bytes 98304
  821.2 61.8 %reduce-scatter.10.cloned.1.call-done = f32[32,1024]{1,0:T(8,128)} async-done(((f32[1024,1024]{1,0:T(8,128)}), f32[32,1024]{1,0:T(8,128)}) %reduce-scatter.10.cloned.1.call-update) | async-done | bytes 131088 | tf_op jit(solution)/shard_map/reduce_scatter | solution.py:302
  883.1 365.9 %reduce-scatter.12.cloned.1.call-done = f32[32,4096]{1,0:T(8,128)} async-done(((f32[1024,4096]{1,0:T(8,128)}), f32[32,4096]{1,0:T(8,128)}) %reduce-scatter.12.cloned.1.call-update) | async-done | bytes 524304 | tf_op jit(solution)/shard_map/reduce_scatter | solution.py:304
  1249.0 365.0 %reduce-scatter.14.cloned.1.call-done = f32[128,1024]{1,0:T(8,128)} async-done(((f32[4096,1024]{1,0:T(8,128)}), f32[128,1024]{1,0:T(8,128)}) %reduce-scatter.14.cloned.1.call-update) | async-done | bytes 524304 | tf_op jit(solution)/shard_map/reduce_scatter | solution.py:306
  1614.0 161.3 %reduce-scatter.8.cloned.1.call-done = f32[32,3072]{1,0:T(8,128)} async-done(((f32[1024,3072]{1,0:T(8,128)}), f32[32,3072]{1,0:T(8,128)}) %reduce-scatter.8.cloned.1.call-update) | async-done | bytes 393232 | tf_op jit(solution)/shard_map/reduce_scatter | solution.py:299
  (155 shorter events, 27.6 us)
Async XLA Ops:
  7.2 31.2 %copy-start = (bf16[1024,1024]{1,0:T(8,128)(2,1)S(1)}, bf16[1024,1024]{1,0:T(8,128)(2,1)}, u32[]{:S(2)}) copy-start(bf16[1024,1024]{1,0:T(8,128)(2,1)} %param.31) | copy-start | bytes 6291460
  7.2 181.8 %all-gather.2.cloned.1.call-start = ((), (), s32[]{:S(2)}) async-start(), calls=%async_computation.5 | async-start | bytes 10485760 | tf_op jit(solution)/shard_map/all_gather | solution.py:199
  8.8 7.8 copy-start.21
  10.5 6.2 copy-start.23
  16.7 3.4 copy-start.32
  29.5 1.3 copy-start.17
  36.5 695.1 %reduce-scatter.6.cloned.1.call-start = ((), (), s32[]{:S(2)}) async-start(), calls=%async_computation.6 | async-start | bytes 20971520 | tf_op jit(solution)/shard_map/reduce_scatter | solution.py:275
  208.7 4.0 copy-start.5
  217.4 1.3 copy-start.6
  266.0 4.0 copy-start.1
  270.0 2.8 copy-start.3
  271.5 1.3 copy-start.2
  275.6 607.5 %reduce-scatter.10.cloned.1.call-start = ((), (), s32[]{:S(2)}) async-start(), calls=%async_computation.8 | async-start | bytes 4325376 | tf_op jit(solution)/shard_map/reduce_scatter | solution.py:302
  275.6 5.1 copy-start.4
  275.6 5.1 copy-start.22
  275.6 5.1 copy-start.24
  275.6 5.1 copy-start.25
  275.7 5.1 copy-start.27
  275.7 5.1 copy-start.28
  280.6 968.4 %reduce-scatter.12.cloned.1.call-start = ((), (), s32[]{:S(2)}) async-start(), calls=%async_computation.9 | async-start | bytes 17301504 | tf_op jit(solution)/shard_map/reduce_scatter | solution.py:304
  280.8 27.7 %copy-start.14 = (bf16[1,512,1024]{2,1,0:T(8,128)(2,1)S(1)}, bf16[1,512,1024]{2,1,0:T(8,128)(2,1)}, u32[]{:S(2)}) copy-start(bf16[1,512,1024]{2,1,0:T(8,128)(2,1)} %param.37) | copy-start | bytes 3145732
  321.8 1.9 copy-start.35
  332.1 1281.9 %reduce-scatter.14.cloned.1.call-start = ((), (), s32[]{:S(2)}) async-start(), calls=%async_computation.10 | async-start | bytes 17301504 | tf_op jit(solution)/shard_map/reduce_scatter | solution.py:306
  345.2 388.4 %copy-start.18 = (f32[512,8]{0,1:T(8,128)S(1)}, f32[512,8]{0,1:T(8,128)}, u32[]{:S(2)}) copy-start(f32[512,8]{0,1:T(8,128)} %copy-done.17) | copy-start | bytes 49156
  345.2 388.4 %copy-start.19 = (f32[512,8]{0,1:T(8,128)S(1)}, f32[512,8]{0,1:T(8,128)}, u32[]{:S(2)}) copy-start(f32[512,8]{0,1:T(8,128)} %get-tuple-element.845) | copy-start | bytes 49156
  345.2 1430.1 %reduce-scatter.8.cloned.1.call-start = ((), (), s32[]{:S(2)}) async-start(), calls=%async_computation.7 | async-start | bytes 12976128 | tf_op jit(solution)/shard_map/reduce_scatter | solution.py:299
  347.7 390.8 %copy-start.26 = (f32[1024]{0:T(1024)S(1)}, f32[1024]{0:T(1024)}, u32[]{:S(2)}) copy-start(f32[1024]{0:T(1024)} %param.25) | copy-start | bytes 12292
  347.7 390.8 %copy-start.29 = (f32[1024]{0:T(1024)S(1)}, f32[1024]{0:T(1024)}, u32[]{:S(2)}) copy-start(f32[1024]{0:T(1024)} %param.26) | copy-start | bytes 12292
  731.6 3.2 copy-start.13
  735.0 2.5 copy-start.9
  735.0 2.5 copy-start.11
  737.5 1.0 copy-start.7
  748.1 8.4 copy-start.34
  748.1 19.3 %slice-start.2 = ((s8[6291456]{0:T(1024)(128)(4,1)}), s8[4194304]{0:T(1024)(128)(4,1)S(1)}, s32[]{:S(2)}) async-start(s8[6291456]{0:T(1024)(128)(4,1)} %bitcast.268), calls=%async_computation.13 | async-start | bytes 8388608
  756.5 7.2 copy-start.16
  756.6 7.2 copy-start.30
  756.6 7.2 copy-start.31
  756.6 10.9 slice-start.3
  763.7 2.4 copy-start.8
  763.8 2.4 copy-start.10
  763.8 2.4 copy-start.12
  767.4 4.9 copy-start.20
  767.5 4.9 copy-start.15
  772.3 2.4 slice-start
  772.3 2.4 slice-start.1
  817.7 958.1 %copy-start.33 = (f32[32]{0:T(128)}, f32[32]{0:T(128)S(1)}, u32[]{:S(2)}) copy-start(f32[32]{0:T(128)S(1)} %dynamic-slice.10) | copy-start | bytes 388
Sparse Core Ops, SparseCore 0:
  36.6 152.3 all-gather.1
  275.7 455.9 reduce-scatter.5
  734.6 148.4 reduce-scatter.9
  885.9 363.0 reduce-scatter.11
  1251.8 362.1 reduce-scatter.13
  1621.5 153.7 reduce-scatter.7
where the time goes:
time: 1790 us; the launch traced here: 1780 us
  waiting for transfers between devices  1480 us (83%)
  matrix products  154 us (9%)
  local copies, waits for them, and re-layouts  61.7 us (3%)
  blocking collectives  42.3 us (2%)
  other arithmetic  26.4 us (1%)
    reduce_scatter x1, waiting for transfers between devices, local(): lax.psum_scatter(back_state[1], 'blk', scatter_dimension=1, tiled=True)  384 us
    reduce_scatter x1, waiting for transfers between devices, local(): lax.psum_scatter(expand_grad, ('batch', 'blk'), scatter_dimension=0, tile...  366 us
    reduce_scatter x1, waiting for transfers between devices, local(): lax.psum_scatter(reduce_grad, ('batch', 'blk'), scatter_dimension=0, tile...  365 us
    reduce_scatter x1, waiting for transfers between devices, local(): lax.psum_scatter(joint_grad, ('batch', 'blk'), scatter_dimension=0, tiled...  161 us
    all_gather x1, waiting for transfers between devices, local(): lax.all_gather(pair_local, 'blk', axis=1, tiled=True)  144 us
    reduce_scatter x1, waiting for transfers between devices, local(): lax.psum_scatter(dense_grad, ('batch', 'blk'), scatter_dimension=0, tiled...  61.8 us
    unnamed x1, blocking collectives  42.3 us
  transfers between devices with their start and end apart: 6, of which 6 were waited for; matrix products, arithmetic and copies ran while one was open for 7% of the time, Pallas kernels for 0%

commit v1 on v0

--- a/solution.py
+++ b/solution.py
@@ -3,6 +3,8 @@
 import jax
 import jax.numpy as jnp
 from jax import lax
+from jax.experimental import pallas as pl
+from jax.experimental.pallas import tpu as pltpu
 from jax.sharding import PartitionSpec as P
 
 HEADS = 16
@@ -324,44 +326,981 @@
     )
 
 
+BQ = 512
+N = 4
+TM = 256
+VMEM = 56 * 1024 * 1024
+NEG = -1e30
+NN = (((1,), (0,)), ((), ()))
+NT = (((1,), (1,)), ((), ()))
+TN = (((0,), (0,)), ((), ()))
+
+
+def mm(left, right, form=NN):
+    return lax.dot_general(left, right, form, preferred_element_type=jnp.float32)
+
+
+def low(value):
+    return value.astype(jnp.bfloat16)
+
+
+def wide(value):
+    return value.astype(jnp.float32)
+
+
+def gelu_parts(hidden):
+    size = jnp.abs(hidden) * (0.5**0.5)
+    bell = jnp.exp(-(size * size))
+    base = 1.0 + 0.3275911 * size
+    guess = pl.reciprocal(base, approx=True)
+    t = guess * (2.0 - base * guess)
+    series = t * (
+        0.5 * 0.254829592
+        + t
+        * (
+            0.5 * -0.284496736
+            + t * (0.5 * 1.421413741 + t * (0.5 * -1.453152027 + t * (0.5 * 1.061405429)))
+        )
+    )
+    tail = series * bell
+    return (jnp.where(hidden >= 0.0, 1.0 - tail, tail), bell)
+
+
+def fold_rows(value):
+    rows, columns = value.shape
+    return jnp.sum(value.reshape(rows // 8, 8, columns), axis=0)
+
+
+def prepare_kernel(spot_ref, wj_ref, wd_ref, we_ref, wr_ref, wj_out, wd_out, we_out, wr_out):
+    turned = wj_ref[...].T
+    wj_out[...] = jnp.where(lax.rem(spot_ref[0], 2) == 0, turned[:HEAD], turned[HEAD:])
+    wd_out[...] = wd_ref[...]
+    we_out[...] = we_ref[...]
+    wr_out[...] = wr_ref[...]
+
+
+def prepare(quarter, joint_weight, dense_weight, expand_weight, reduce_weight):
+    width, units = expand_weight.shape
+    heads = HEADS // N
+    groups = units // (N * 128)
+    kinds = 3 * heads
+    pair = lambda s, spot: (0, (s // heads) * (HEADS // 2) + (s % heads) * (N // 2) + spot[0] // 2)
+    row = lambda s: jnp.minimum(s, heads - 1)
+    unit = lambda s: jnp.minimum(s, groups - 1)
+    group = lambda s, spot: N * unit(s) + lax.rem(spot[0] + 2 * lax.rem(unit(s), 2), N)
+    shape = lambda *dims: jax.ShapeDtypeStruct(dims, jnp.bfloat16)
+    return pl.pallas_call(
+        prepare_kernel,
+        grid_spec=pltpu.PrefetchScalarGridSpec(
+            num_scalar_prefetch=1,
+            grid=(kinds,),
+            in_specs=[
+                pl.BlockSpec((width, 2 * HEAD), pair),
+                pl.BlockSpec((HEAD, width), lambda s, spot: (N * row(s) + spot[0], 0)),
+                pl.BlockSpec((width, 128), lambda s, spot: (0, group(s, spot))),
+                pl.BlockSpec((128, width), lambda s, spot: (group(s, spot), 0)),
+            ],
+            out_specs=[
+                pl.BlockSpec((HEAD, width), lambda s, spot: (s, 0)),
+                pl.BlockSpec((HEAD, width), lambda s, spot: (row(s), 0)),
+                pl.BlockSpec((width, 128), lambda s, spot: (0, unit(s))),
+                pl.BlockSpec((128, width), lambda s, spot: (unit(s), 0)),
+            ],
+        ),
+        out_shape=[
+            shape(kinds * HEAD, width),
+            shape(heads * HEAD, width),
+            shape(width, groups * 128),
+            shape(groups * 128, width),
+        ],
+        cost_estimate=pl.CostEstimate(flops=0, bytes_accessed=14 * width * width, transcendentals=0),
+    )(quarter.reshape(1), joint_weight, dense_weight, expand_weight, reduce_weight)
+
+
+def block_at(place, j):
+    return place * (place + 1) // 2 + j
+
+
+def forward_kernel(held, qkv_ref, kx_ref, qx_ref, *refs):
+    mixed_ref, full_ref, inverse_ref, share_ref, key_ref, *scores = refs[held:]
+    key_ref[...] = jnp.concatenate([qkv_ref[1, 0], kx_ref[...]], axis=0).T
+    total = kx_ref.shape[1]
+    state = {}
+
+    def score(place, j):
+        here = slice(place * BQ, (place + 1) * BQ)
+        at = slice(j * BQ, (j + 1) * BQ)
+        if j == 0:
+            query_x = jnp.concatenate([qkv_ref[0, 0, :, here], qx_ref[:, here]], axis=0)
+            state[place] = [query_x, jnp.full((8, BQ), NEG * 2, jnp.float32)]
+        found = mm(key_ref[at, :], state[place][0])
+        if j == place:
+            key_row = lax.broadcasted_iota(jnp.int32, (BQ, BQ), 0)
+            query_column = lax.broadcasted_iota(jnp.int32, (BQ, BQ), 1)
+            found = jnp.where(key_row <= query_column, found, NEG)
+        scores[place % 2][at, :] = found
+        state[place][1] = jnp.maximum(state[place][1], jnp.max(found.reshape(BQ // 8, 8, BQ), axis=0))
+
+    def weigh(place, j):
+        here = slice(place * BQ, (place + 1) * BQ)
+        at = slice(j * BQ, (j + 1) * BQ)
+        if j == 0:
+            peak = jnp.max(state[place][1], axis=0, keepdims=True)
+            state[place] = [peak, jnp.zeros((8, BQ), jnp.float32), jnp.zeros((HEAD, BQ), jnp.float32)]
+        share = jnp.exp(scores[place % 2][at, :] - state[place][0])
+        state[place][1] = state[place][1] + jnp.sum(share.reshape(BQ // 8, 8, BQ), axis=0)
+        share = low(share)
+        share_ref[0, block_at(place, j)] = share
+        state[place][2] = state[place][2] + mm(qkv_ref[2, 0, :, at], share)
+        if j == place:
+            inverse = 1.0 / jnp.sum(state[place][1], axis=0, keepdims=True)
+            mixed = state[place][2] * inverse
+            inverse_ref[0, :, here] = inverse
+            full_ref[0, :, here] = mixed
+            mixed_ref[0, :, here] = low(mixed)
+
+    places = list(range(total // BQ))
+    for j in range(places[0] + 1):
+        score(places[0], j)
+    for n, place in enumerate(places):
+        for j in range(places[-1] + 2):
+            if n + 1 < len(places) and j <= places[n + 1]:
+                score(places[n + 1], j)
+            if j <= place:
+                weigh(place, j)
+
+
+def attend_forward(qkv, kx, qx, first, count, before):
+    _, heads, _, total = qkv.shape
+    places = total // BQ
+    blocks = block_at(places, 0)
+    head_rows = lambda rows: pl.BlockSpec((1, rows, total), lambda h: (first + h, 0, 0))
+    operands = [qkv, kx, qx]
+    in_specs = [
+        pl.BlockSpec((3, 1, HEAD, total), lambda h: (0, first + h, 0, 0)),
+        pl.BlockSpec((HEAD, total), lambda h: (0, 0)),
+        pl.BlockSpec((HEAD, total), lambda h: (0, 0)),
+    ]
+    aliases = {}
+    if before is not None:
+        for index, array in enumerate(before):
+            aliases[len(operands)] = index
+            operands.append(array)
+            in_specs.append(pl.BlockSpec(memory_space=pl.ANY))
+    return pl.pallas_call(
+        partial(forward_kernel, len(aliases)),
+        grid=(count,),
+        in_specs=in_specs,
+        out_specs=[
+            head_rows(HEAD),
+            head_rows(HEAD),
+            head_rows(1),
+            pl.BlockSpec((1, blocks, BQ, BQ), lambda h: (first + h, 0, 0, 0)),
+        ],
+        out_shape=[
+            jax.ShapeDtypeStruct((heads, HEAD, total), jnp.bfloat16),
+            jax.ShapeDtypeStruct((heads, HEAD, total), jnp.float32),
+            jax.ShapeDtypeStruct((heads, 1, total), jnp.float32),
+            jax.ShapeDtypeStruct((heads, blocks, BQ, BQ), jnp.bfloat16),
+        ],
+        scratch_shapes=[pltpu.VMEM((total, 2 * HEAD), jnp.bfloat16)] + [pltpu.VMEM((total, BQ), jnp.float32)] * 2,
+        input_output_aliases=aliases,
+        compiler_params=pltpu.CompilerParams(vmem_limit_bytes=VMEM),
+        cost_estimate=pl.CostEstimate(
+            flops=16 * HEAD * count * blocks * BQ * BQ,
+            bytes_accessed=2 * count * blocks * BQ * BQ,
+            transcendentals=count * blocks * BQ * BQ,
+        ),
+    )(*operands)
+
+
+def backward_kernel(qkv_ref, mg_ref, full_ref, inverse_ref, share_ref, cos_ref, sin_ref, jb_ref, value_ref, acc_ref):
+    total = cos_ref.shape[1]
+    ones = (lax.broadcasted_iota(jnp.int32, (HEAD, total), 0) < 3).astype(jnp.bfloat16)
+    value_ref[...] = jnp.concatenate([qkv_ref[2, 0], ones], axis=0).T
+    half = ROTARY // 2
+    blank = jnp.zeros((HEAD, BQ), jnp.bfloat16)
+    row = lax.broadcasted_iota(jnp.int32, (HEAD, BQ), 0)
+
+    def turn_back(rows, at):
+        lead, tail = rows[:half], rows[half : 2 * half]
+        cosine, sine = cos_ref[:, at], sin_ref[:, at]
+        return low(
+            jnp.concatenate([lead * cosine + tail * sine, tail * cosine - lead * sine, rows[2 * half :]], axis=0)
+        )
+
+    for place in reversed(range(total // BQ)):
+        here = slice(place * BQ, (place + 1) * BQ)
+        query_t = qkv_ref[0, 0, :, here]
+        mg = low(wide(mg_ref[0, :, here]) * inverse_ref[0, :, here])
+        delta = -jnp.sum(wide(mg) * full_ref[0, :, here], axis=0, keepdims=True)
+        first = low(delta)
+        rest = delta - wide(first)
+        middle = low(rest)
+        final = low(rest - wide(middle))
+        extra = jnp.where(
+            row == 0, wide(first), jnp.where(row == 1, wide(middle), jnp.where(row == 2, wide(final), 0.0))
+        )
+        mg_x = jnp.concatenate([mg, low(extra)], axis=0)
+        mg_v = jnp.concatenate([blank, mg], axis=0)
+        query_k = jnp.concatenate([query_t, blank], axis=0)
+        query_grad = jnp.zeros((HEAD, BQ), jnp.float32)
+        for j in range(place + 1):
+            at = slice(j * BQ, (j + 1) * BQ)
+            share = share_ref[0, block_at(place, j)]
+            score_grad = low(wide(share) * mm(value_ref[at, :], mg_x))
+            pair = mm(share, mg_v, NT) + mm(score_grad, query_k, NT)
+            query_grad = query_grad + mm(qkv_ref[1, 0, :, at], score_grad)
+            if (place + 1) * BQ < total:
+                pair = pair + acc_ref[at, :]
+            if j < place:
+                acc_ref[at, :] = pair
+            else:
+                pair_t = pair.T
+                jb_ref[1, 0, :, at] = turn_back(pair_t[:HEAD], at)
+                jb_ref[2, 0, :, at] = low(pair_t[HEAD:])
+        jb_ref[0, 0, :, here] = turn_back(query_grad * (HEAD**-0.5), here)
+
+
+def attend_backward(qkv, mg, full, inverse, shares, tables):
+    _, heads, _, total = qkv.shape
+    blocks = shares.shape[1]
+    head_rows = lambda rows: pl.BlockSpec((1, rows, total), lambda h: (h, 0, 0))
+    kinds = pl.BlockSpec((3, 1, HEAD, total), lambda h: (0, h, 0, 0))
+    table = pl.BlockSpec((ROTARY // 2, total), lambda h: (0, 0))
+    return pl.pallas_call(
+        backward_kernel,
+        grid=(heads,),
+        in_specs=[
+            kinds,
+            head_rows(HEAD),
+            head_rows(HEAD),
+            head_rows(1),
+            pl.BlockSpec((1, blocks, BQ, BQ), lambda h: (h, 0, 0, 0)),
+            table,
+            table,
+        ],
+        out_specs=kinds,
+        out_shape=jax.ShapeDtypeStruct((3, heads, HEAD, total), jnp.bfloat16),
+        scratch_shapes=[
+            pltpu.VMEM((total, 2 * HEAD), jnp.bfloat16),
+            pltpu.VMEM((total, 2 * HEAD), jnp.float32),
+        ],
+        compiler_params=pltpu.CompilerParams(vmem_limit_bytes=VMEM),
+        cost_estimate=pl.CostEstimate(
+            flops=32 * HEAD * heads * blocks * BQ * BQ,
+            bytes_accessed=2 * heads * blocks * BQ * BQ,
+            transcendentals=0,
+        ),
+    )(qkv, mg, full, inverse, shares, *tables)
+
+
+def token_kernel(count, sub, chunk, spot_ref, *refs):
+    a_ref, b_ref = refs[0], refs[count - 1]
+    (wj_ref, bj_ref, we_ref, be_ref, wr_ref, g1_ref, s1_ref, g2_ref, s2_ref, cos_ref, sin_ref) = refs[count : count + 11]
+    qkv_ref, unit_ref, second_ref, active_ref, slope_ref, feed_ref = refs[-6:]
+    step = pl.program_id(0)
+    pick_b = spot_ref[pl.num_programs(0) + step] == 1
+    rows = a_ref.shape[0]
+    half = ROTARY // 2
+    part = wj_ref.shape[0] // 3
+    for top in range(0, rows, sub):
+        at = slice(top, top + sub)
+        x = wide(a_ref[at, :] if count == 1 else jnp.where(pick_b, b_ref[at, :], a_ref[at, :]))
+        center = x - jnp.mean(x, axis=-1, keepdims=True)
+        scale = lax.rsqrt(jnp.mean(center * center, axis=-1, keepdims=True) + EPSILON)
+        unit = center * scale
+        unit_ref[at, :] = low(unit)
+        normed = low(unit * g1_ref[...] + s1_ref[...])
+        second = low(unit * g2_ref[...] + s2_ref[...])
+        second_ref[at, :] = second
+        joint = mm(wj_ref[...], normed, NT) + bj_ref[...]
+        cosine, sine = cos_ref[:, at], sin_ref[:, at]
+        for kind in range(3):
+            for head in range(part // HEAD):
+                first = kind * part + head * HEAD
+                turned = joint[first : first + HEAD]
+                if kind < 2:
+                    lead, tail = turned[:half], turned[half : 2 * half]
+                    turned = jnp.concatenate(
+                        [lead * cosine - tail * sine, tail * cosine + lead * sine, turned[2 * half :]], axis=0
+                    )
+                if kind == 0:
+                    turned = turned * (HEAD**-0.5)
+                qkv_ref[first : first + HEAD, at] = low(turned)
+        for left in range(0, we_ref.shape[1], chunk):
+            over = slice(left, left + chunk)
+            hidden = mm(second, we_ref[:, over]) + be_ref[:, over]
+            share, bell = gelu_parts(hidden)
+            active_ref[at, over] = low(hidden * share)
+            slope_ref[at, over] = low(share + hidden * bell * 0.3989422804014327)
+    for top in range(0, rows, sub):
+        at = slice(top, top + sub)
+        feed_ref[at, :] = low(mm(active_ref[at, :], wr_ref[...]))
+
+
+def run_tokens(slot, spot, a, b, weights, tables, before, sub=256, chunk=256):
+    rows, width = a.shape
+    total = tables[0].shape[1]
+    wj, bj, we, be, wr, g1, s1, g2, s2 = weights
+    units = we.shape[1]
+    steps = spot.shape[0] // 2
+
+    def whole(array):
+        return pl.BlockSpec(array.shape, lambda i, spot: (0,) * array.ndim)
+
+    column = lambda height: pl.BlockSpec((height, rows), lambda i, spot: (0, spot[i]))
+    placed = pl.BlockSpec((rows, width), lambda i, spot: (spot[i], 0))
+    arrived = lambda size: pl.BlockSpec((rows, size), lambda i, spot: (slot + i, 0))
+    data = [a] if a is b else [a, b]
+    in_specs = [whole(w) for w in (*data, *weights)] + [column(ROTARY // 2)] * 2
+    out_specs = [column(wj.shape[0]), placed, arrived(width), arrived(units), arrived(units), placed]
+    shape = lambda *dims: jax.ShapeDtypeStruct(dims, jnp.bfloat16)
+    out_shape = [shape(wj.shape[0], total)] + [shape(total, size) for size in (width, width, units, units, width)]
+    operands = [spot, *data, *weights, *tables]
+    aliases = {}
+    if before is not None:
+        for index, array in enumerate(before):
+            aliases[len(operands)] = index
+            operands.append(array)
+            in_specs.append(pl.BlockSpec(memory_space=pl.ANY))
+    products = steps * rows * width * (wj.shape[0] + 2 * units)
+    return pl.pallas_call(
+        partial(token_kernel, len(data), sub, chunk),
+        grid_spec=pltpu.PrefetchScalarGridSpec(
+            num_scalar_prefetch=1, grid=(steps,), in_specs=in_specs, out_specs=out_specs
+        ),
+        out_shape=out_shape,
+        input_output_aliases=aliases,
+        compiler_params=pltpu.CompilerParams(vmem_limit_bytes=VMEM),
+        cost_estimate=pl.CostEstimate(
+            flops=4 * products, bytes_accessed=16 * steps * rows * width, transcendentals=steps * rows * units
+        ),
+    )(*operands)
+
+
+def upstream_kernel(chunk, spot_ref, *refs):
+    sources = refs[:6]
+    (wd_ref, we_ref, wr_ref, g2_ref, unit_ref, slope_ref) = refs[6:12]
+    (mg_ref, back_ref, up_ref, hg_ref, sums_ref, hsum_ref) = refs[12:18]
+    buffer, sems = refs[18:]
+    step = pl.program_id(0)
+    steps = pl.num_programs(0)
+    slot = lax.rem(step, 2)
+
+    def fetch(which, into):
+        for k, source in enumerate(sources):
+
+            @pl.when(spot_ref[steps + which] == k)
+            def _():
+                pltpu.make_async_copy(source, buffer.at[into], sems.at[into]).start()
+
+    @pl.when(step == 0)
+    def _():
+        fetch(0, 0)
+        sums_ref[...] = jnp.zeros_like(sums_ref)
+        hsum_ref[...] = jnp.zeros_like(hsum_ref)
+
+    @pl.when(step + 1 < steps)
+    def _():
+        fetch(step + 1, 1 - slot)
+
+    pltpu.make_async_copy(sources[0], buffer.at[slot], sems.at[slot]).wait()
+    up = buffer[slot]
+    up_ref[...] = up
+    mg_ref[...] = low(mm(wd_ref[...], up, NT))
+    for left in range(0, we_ref.shape[1], chunk):
+        over = slice(left, left + chunk)
+        piece = low(mm(up, wr_ref[over, :], NT) * wide(slope_ref[:, over]))
+        hg_ref[:, over] = piece
+        hsum_ref[:, over] += fold_rows(wide(piece))
+    for left in range(0, we_ref.shape[0], chunk):
+        over = slice(left, left + chunk)
+        back = mm(hg_ref[...], we_ref[over, :], NT)
+        back_ref[:, over] = low(back * g2_ref[:, over])
+        sums_ref[0, :, over] += fold_rows(back * wide(unit_ref[:, over]))
+        sums_ref[1, :, over] += fold_rows(back)
+
+
+def run_upstream(spot, sources, weights, unit, slope, chunk=256):
+    rows, width = sources[0].shape
+    total = unit.shape[0]
+    wd, we, wr, g2 = weights
+    units = we.shape[1]
+    steps = total // rows
+
+    def whole(array):
+        return pl.BlockSpec(array.shape, lambda i, spot: (0,) * array.ndim)
+
+    fixed = lambda *dims: pl.BlockSpec(dims, lambda i, spot: (0,) * len(dims))
+    column = lambda height: pl.BlockSpec((height, rows), lambda i, spot: (0, spot[i]))
+    placed = pl.BlockSpec((rows, width), lambda i, spot: (spot[i], 0))
+    arrived = lambda size: pl.BlockSpec((rows, size), lambda i, spot: (i, 0))
+    in_specs = [pl.BlockSpec(memory_space=pl.ANY)] * 6 + [whole(w) for w in weights] + [placed, arrived(units)]
+    out_specs = [column(wd.shape[0]), placed, arrived(width), arrived(units), fixed(2, 8, width), fixed(8, units)]
+    shape = lambda *dims: jax.ShapeDtypeStruct(dims, jnp.bfloat16)
+    out_shape = [
+        shape(wd.shape[0], total),
+        shape(total, width),
+        shape(total, width),
+        shape(total, units),
+        jax.ShapeDtypeStruct((2, 8, width), jnp.float32),
+        jax.ShapeDtypeStruct((8, units), jnp.float32),
+    ]
+    return pl.pallas_call(
+        partial(upstream_kernel, chunk),
+        grid_spec=pltpu.PrefetchScalarGridSpec(
+            num_scalar_prefetch=1,
+            grid=(steps,),
+            in_specs=in_specs,
+            out_specs=out_specs,
+            scratch_shapes=[
+                pltpu.VMEM((2, rows, width), jnp.bfloat16),
+                pltpu.SemaphoreType.DMA((2,)),
+            ],
+        ),
+        out_shape=out_shape,
+        compiler_params=pltpu.CompilerParams(vmem_limit_bytes=VMEM),
+        cost_estimate=pl.CostEstimate(
+            flops=3 * total * width * (wd.shape[0] + 2 * units), bytes_accessed=12 * total * width, transcendentals=0
+        ),
+    )(spot, *sources, wd, we, wr, g2, unit, slope)
+
+
+def weight_kernel(spot_ref, second_ref, hg_ref, active_ref, up_ref, mixed_ref, *refs):
+    shares, (expand_sum, reduce_sum, dense_sum) = refs[:4], refs[4:]
+    step = pl.program_id(0)
+    steps = pl.num_programs(0)
+
+    @pl.when(step == 0)
+    def _():
+        expand_sum[...] = jnp.zeros_like(expand_sum)
+        reduce_sum[...] = jnp.zeros_like(reduce_sum)
+        dense_sum[...] = jnp.zeros_like(dense_sum)
+
+    up = up_ref[...]
+    dense_sum[...] += mm(mixed_ref[...], up)
+    expand_sum[...] += mm(second_ref[...], hg_ref[...], TN)
+    reduce_sum[...] += mm(active_ref[...], up, TN)
+
+    @pl.when(step == steps - 1)
+    def _():
+        col = spot_ref[steps]
+        large, small = expand_sum.shape[0] // 4, dense_sum.shape[0] // 4
+        for k, share in enumerate(shares):
+            i = k + col - 2 * (col & k)
+            at = pl.ds(pl.multiple_of(i * large, large), large)
+            share[:large] = low(expand_sum[at, :])
+            share[large : 2 * large] = low(reduce_sum[at, :])
+            share[2 * large :] = low(dense_sum[pl.ds(pl.multiple_of(i * small, small), small), :])
+
+
+def weight_gradients(spot, second, hg, active, ups, mixed):
+    total, width = second.shape
+    units = hg.shape[1]
+    rows = total // N
+    height = mixed.shape[0]
+    fixed = lambda *dims: pl.BlockSpec(dims, lambda i, spot: (0,) * len(dims))
+    arrived = lambda size: pl.BlockSpec((rows, size), lambda i, spot: (i, 0))
+    dims = (width // 4 + units // 4 + height // 4, width)
+    return pl.pallas_call(
+        weight_kernel,
+        grid_spec=pltpu.PrefetchScalarGridSpec(
+            num_scalar_prefetch=1,
+            grid=(N,),
+            in_specs=[
+                arrived(width),
+                arrived(units),
+                arrived(units),
+                arrived(width),
+                pl.BlockSpec((height, rows), lambda i, spot: (0, spot[i])),
+            ],
+            out_specs=[fixed(*dims)] * 4,
+            scratch_shapes=[
+                pltpu.VMEM((width, units), jnp.float32),
+                pltpu.VMEM((units, width), jnp.float32),
+                pltpu.VMEM((height, width), jnp.float32),
+            ],
+        ),
+        out_shape=[jax.ShapeDtypeStruct(dims, jnp.bfloat16)] * 4,
+        compiler_params=pltpu.CompilerParams(vmem_limit_bytes=VMEM),
+        cost_estimate=pl.CostEstimate(
+            flops=3 * total * width * (height + 2 * units), bytes_accessed=8 * total * width, transcendentals=0
+        ),
+    )(spot, second, hg, active, ups, mixed)
+
+
+def deliver_kernel(order_ref, left_ref, weight_ref, add_ref, *refs):
+    del order_ref
+    send_ref, keep_ref = refs[-2:]
+    step = pl.program_id(0)
+    value = mm(left_ref[...], weight_ref[...], TN)
+    if len(refs) > 2:
+        value = value * refs[0][...]
+    value = low(value + wide(add_ref[...]))
+
+    @pl.when(step < pl.num_programs(0) // 2)
+    def _():
+        send_ref[...] = value
+
+    @pl.when(step >= pl.num_programs(0) // 2)
+    def _():
+        keep_ref[...] = value
+
+
+def deliver(order, left, weight, add, gain=None):
+    depth, total = left.shape
+    width = weight.shape[1]
+    steps = N
+    tile = total // N
+    rows = pl.BlockSpec((tile, width), lambda s, order: (order[s], 0))
+    in_specs = [
+        pl.BlockSpec((depth, tile), lambda s, order: (0, order[s])),
+        pl.BlockSpec((depth, width), lambda s, order: (0, 0)),
+        rows,
+    ]
+    operands = [left, weight, add]
+    if gain is not None:
+        in_specs.append(pl.BlockSpec((1, width), lambda s, order: (0, 0)))
+        operands.append(gain)
+    return pl.pallas_call(
+        deliver_kernel,
+        grid_spec=pltpu.PrefetchScalarGridSpec(
+            num_scalar_prefetch=1,
+            grid=(steps,),
+            in_specs=in_specs,
+            out_specs=[
+                pl.BlockSpec((tile, width), lambda s, order: (jnp.minimum(s, steps // 2 - 1), 0)),
+                pl.BlockSpec((tile, width), lambda s, order: (jnp.maximum(s - steps // 2, 0), 0)),
+            ],
+        ),
+        out_shape=[jax.ShapeDtypeStruct((total // 2, width), jnp.bfloat16)] * 2,
+        compiler_params=pltpu.CompilerParams(vmem_limit_bytes=VMEM),
+        cost_estimate=pl.CostEstimate(
+            flops=0, bytes_accessed=0, transcendentals=0
+        ),
+    )(order, *operands)
+
+
+def joint_kernel(spot_ref, jb_ref, unit_ref, wj_ref, gain_ref, shift_ref, sums_ref, up_ref, hsum_ref, *refs):
+    shares, (vector_ref, total_ref, turned_ref, sum_ref) = refs[:4], refs[4:]
+    step = pl.program_id(0)
+    jb = jb_ref[...]
+    height, tile = jb.shape
+    width = unit_ref.shape[1]
+
+    @pl.when(step == 0)
+    def _():
+        total_ref[...] = jnp.zeros_like(total_ref)
+        sum_ref[...] = jnp.zeros_like(sum_ref)
+
+    total_ref[...] += mm(jb, unit_ref[...])
+    sum_ref[...] += mm(jb, jnp.ones((tile, 128), jnp.bfloat16))
+
+    @pl.when(step == pl.num_programs(0) - 1)
+    def _():
+        col, quarter = spot_ref[0], spot_ref[1]
+        gain = jnp.sum(total_ref[...] * wide(wj_ref[...]), axis=0, keepdims=True)
+        turned_ref[...] = (total_ref[...] * gain_ref[...] + sum_ref[:, :1] * shift_ref[...]).T
+        part = width // 4
+        for k, share in enumerate(shares):
+            i = k + col - 2 * (col & k)
+            share[:part] = low(turned_ref[pl.ds(pl.multiple_of(i * part, part), part), :])
+        jb_sum = sum_ref[...].T[:1]
+        first = low(jb_sum)
+        rest = jb_sum - wide(first)
+        middle = low(rest)
+        final = low(rest - wide(middle))
+        shift = mm(jnp.concatenate([first, middle, final], axis=0), wj_ref[...])
+        rows = [
+            gain,
+            jnp.sum(shift, axis=0, keepdims=True),
+            jnp.sum(sums_ref[0], axis=0, keepdims=True),
+            jnp.sum(sums_ref[1], axis=0, keepdims=True),
+            jnp.sum(up_ref[...], axis=0, keepdims=True),
+        ]
+        jb_sum = jnp.concatenate([jb_sum, jnp.zeros((1, width - height), jnp.float32)], axis=1)
+        for whole in (jnp.sum(hsum_ref[...], axis=0, keepdims=True), jb_sum):
+            rows += [jnp.where(quarter == i, whole, 0.0) for i in range(N)]
+        rows.append(jnp.zeros((3, width), jnp.float32))
+        vector = jnp.concatenate(rows, axis=0)
+        vector_ref[...] = vector
+        coarse = low(vector)
+        fine = low(vector - wide(coarse))
+        rest = jnp.zeros((16, 2 * height - width), jnp.bfloat16)
+        pieces = [coarse[:, :height], fine[:, :height]]
+        pieces += [jnp.concatenate([piece[:, height:], rest], axis=1) for piece in (coarse, fine)]
+        for share in shares[1:]:
+            for n, piece in enumerate(pieces):
+                share[part + 16 * n : part + 16 * (n + 1)] = piece
+
+
+def joint_gradient(spot, jb, unit, wj, gain, shift, sums, up_sum, hsum):
+    height, total = jb.shape
+    width = unit.shape[1]
+    tile = total // N
+    fixed = lambda *dims: pl.BlockSpec(dims, lambda s, spot: (0,) * len(dims))
+    shapes = [(width // 4, height)] + [(width // 4 + 64, height)] * 3
+    return pl.pallas_call(
+        joint_kernel,
+        grid_spec=pltpu.PrefetchScalarGridSpec(
+            num_scalar_prefetch=1,
+            grid=(N,),
+            in_specs=[
+                pl.BlockSpec((height, tile), lambda s, spot: (0, s)),
+                pl.BlockSpec((tile, width), lambda s, spot: (s, 0)),
+                fixed(height, width),
+                fixed(1, width),
+                fixed(1, width),
+                fixed(2, 8, width),
+                fixed(8, width),
+                fixed(*hsum.shape),
+            ],
+            out_specs=[fixed(*dims) for dims in shapes] + [fixed(16, width)],
+            scratch_shapes=[
+                pltpu.VMEM((height, width), jnp.float32),
+                pltpu.VMEM((width, height), jnp.float32),
+                pltpu.VMEM((height, 128), jnp.float32),
+            ],
+        ),
+        out_shape=[jax.ShapeDtypeStruct(dims, jnp.bfloat16) for dims in shapes]
+        + [jax.ShapeDtypeStruct((16, width), jnp.float32)],
+        compiler_params=pltpu.CompilerParams(vmem_limit_bytes=VMEM),
+        cost_estimate=pl.CostEstimate(
+            flops=0, bytes_accessed=0, transcendentals=0
+        ),
+    )(spot, jb, unit, wj, gain, shift, sums, up_sum, hsum)
+
+
+def pack(vector, width):
+    coarse = low(vector)
+    fine = low(vector - wide(coarse))
+    rest = jnp.zeros((vector.shape[0], 2 * width - vector.shape[1]), jnp.bfloat16)
+    pieces = [coarse[:, :width], fine[:, :width]]
+    pieces += [jnp.concatenate([piece[:, width:], rest], axis=1) for piece in (coarse, fine)]
+    return jnp.concatenate(pieces, axis=0)
+
+
+def unpack(rows, size):
+    rows = wide(rows).reshape(4, 16, -1)
+    return jnp.concatenate([rows[0] + rows[1], (rows[2] + rows[3])[:, : size - rows.shape[2]]], axis=1)
+
+
+def hop(value, pairs):
+    return lax.ppermute(value, ("core", "blk"), [(a[0] * N + a[1], b[0] * N + b[1]) for a, b in pairs])
+
+
+PLACES = [(c, z) for c in range(2) for z in range(N)]
+MAIN = [(z // 2, z) for z in range(N)]
+CORE_SWAP = [((c, z), (1 - c, z)) for c, z in PLACES]
+NEAR_SWAP = [((c, z), (c, z ^ 1)) for c, z in PLACES]
+FAR_SWAP = [((c, z), (c, z ^ 2)) for c, z in PLACES]
+FAR_HOME = [((c, z), (1 - c, z ^ 2)) for c, z in PLACES if c != z // 2]
+
+
+HOME = [((c, z), (c, z ^ 1)) for c, z in MAIN] + FAR_HOME
+OFF_MAIN = [(c, z) for c, z in PLACES if c != z // 2]
+FROM_MAIN = [((c, z), (1 - c, z)) for c, z in MAIN]
+TO_MAIN = [((c, z), (1 - c, z)) for c, z in OFF_MAIN]
+NEAR_OFF = [((c, z), (c, z ^ 1)) for c, z in OFF_MAIN]
+
+
+def tie(*arrays):
+    return lax.optimization_barrier(arrays)
+
+
+def near_sum(keep, got):
+    rows = keep.shape[0] // 2
+    return low(wide(keep[rows:]) + wide(got[rows:]))
+
+
+def home_sum(keep, got, near, got_near, main):
+    rows = keep.shape[0] // 2
+    return jnp.where(main, near, low(wide(keep[:rows]) + wide(got[:rows]) + wide(got_near)))
+
+
+def own_sum(keep, got, got_home, main):
+    rows = keep.shape[0] // 2
+    return jnp.where(main, wide(keep[:rows]) + wide(got[:rows]), 0.0) + wide(got_home)
+
+
+def pick(value, axis, index):
+    return lax.dynamic_index_in_dim(value, index, axis, keepdims=False)
+
+
+def plane(values):
+    return [lax.ppermute(value, "col", [(i, i ^ (k + 1)) for i in range(4)]) for k, value in enumerate(values)]
+
+
+NEAR = [((c, z), (c, z ^ 1)) for c, z in PLACES]
+
+
+def first_pieces(value, near):
+    return pick(value, 1, 1 - near).reshape(-1, value.shape[-1])
+
+
+def second_pieces(value, got, core, near):
+    got = got.reshape((2,) + value.shape[2:])
+    return jnp.concatenate([pick(pick(value, 1, near), 0, 1 - core), pick(got, 0, 1 - core)], axis=0)
+
+
+def own_pieces(value, got, last, core, near):
+    got = got.reshape((2,) + value.shape[2:])
+    last = last.reshape((2,) + value.shape[2:])
+    return [pick(pick(value, 1, near), 0, core), last[0], pick(got, 0, core), last[1]]
+
+
+def by_quarter(pieces, quarter, rows):
+    stacked = jnp.stack([piece[:rows] for piece in pieces])
+    return jnp.stack([pick(stacked, 0, quarter ^ k) for k in range(N)])
+
+
+def split_local(
+    tokens,
+    lengths,
+    first_gain,
+    first_shift,
+    second_gain,
+    second_shift,
+    joint_weight,
+    joint_bias,
+    dense_weight,
+    dense_bias,
+    expand_weight,
+    expand_bias,
+    reduce_weight,
+    reduce_bias,
+    cotangent,
+):
+    col, core, z = lax.axis_index("col"), lax.axis_index("core"), lax.axis_index("blk")
+    half, near = z // 2, z % 2
+    quarter = 2 * near + core
+    main = core == half
+    flag = main.astype(jnp.int32)
+    rows, width = tokens.shape[1:]
+    total = rows * N
+    units = expand_weight.shape[1]
+    groups = units // (N * 128)
+    heads = HEADS // N
+    own_x, own_g = tokens[0], cotangent[0]
+    row_of = lambda vector: vector.reshape(1, -1)
+
+    x_other = hop(own_x, FROM_MAIN)
+    x_first = hop(own_x, HOME)
+
+    wj, wd, we, wr = prepare(quarter, joint_weight, dense_weight, expand_weight, reduce_weight)
+    bj = pick(joint_bias.reshape(3, heads, N, HEAD), 2, quarter).reshape(-1, 1)
+    be = expand_bias.reshape(groups // 2, 2, N, 128)
+    be = jnp.stack([pick(be[:, 0], 1, quarter), pick(be[:, 1], 1, quarter ^ 2)], axis=1).reshape(1, -1)
+    first_row, second_row = row_of(first_gain), row_of(second_gain)
+
+    weights = [wj, bj, we, be, wr, first_row, row_of(first_shift), second_row, row_of(second_shift)]
+
+    sizes = jnp.where(main, lengths, hop(lengths, CORE_SWAP))
+    number, offset = doc_tables(sizes, jnp.arange(total, dtype=jnp.int32))
+    inverse = 10000.0 ** (-2.0 * jnp.arange(ROTARY // 2, dtype=jnp.float32) / ROTARY)
+    phase = inverse[:, None] * offset.astype(jnp.float32)
+    tables = [jnp.cos(phase), jnp.sin(phase)]
+    docs = lengths.shape[1]
+    same = number == jnp.arange(HEAD, dtype=jnp.int32)[:, None]
+    used = jnp.arange(HEAD)[:, None] < docs
+    qx = low(jnp.where(same & used, 1.0, 0.0))
+    kx = low(jnp.where(used & ~same, NEG, 0.0))
+
+    spots = [z, z ^ (2 - flag), z ^ (1 + flag), z ^ 3]
+    zero, one = jnp.int32(0), jnp.int32(1)
+    state = run_tokens(0, jnp.stack([spots[0], 1 - flag]), own_x, x_other, weights, tables, None)
+    x_first, *state = tie(x_first, *state)
+    x_first_other = hop(x_first, CORE_SWAP)
+    x_second = hop(x_first, NEAR_OFF)
+    state = run_tokens(1, jnp.stack([spots[1], zero]), x_first, x_first, weights, tables, state)
+    x_first_other, x_second, own_g_late, *state = tie(x_first_other, x_second, own_g, *state)
+    g_first = hop(own_g_late, HOME)
+    g_other = hop(own_g_late, FROM_MAIN)
+    x_second_other = hop(x_second, TO_MAIN)
+    state = run_tokens(2, jnp.stack([spots[2], zero]), x_first_other, x_first_other, weights, tables, state)
+    state = run_tokens(3, jnp.stack([spots[3], 1 - flag]), x_second_other, x_second, weights, tables, state)
+    qkv, unit, second, active, slope, feed = state
+    order = z ^ (jnp.arange(N, dtype=jnp.int32) ^ (2 * flag))
+    qkv = qkv.reshape(3, heads, HEAD, total)
+    attended = attend_forward(qkv, kx, qx, 0, heads // 2, None)
+    g_first, *attended = tie(g_first, *attended)
+    g_second = hop(g_first, NEAR_OFF)
+    g_first_other = hop(g_first, CORE_SWAP)
+    mixed, full, inverse_sum, shares = attend_forward(qkv, kx, qx, heads // 2, heads // 2, attended)
+    mixed = mixed.reshape(-1, total)
+    out_send, out_keep = deliver(order, mixed, wd, feed)
+    g_second, out_send, out_keep = tie(g_second, out_send, out_keep)
+
+    spot = jnp.stack([*spots, 1 - flag, 2 * one, 3 * one, 5 - flag])
+    spot, out_send, out_keep = tie(spot, out_send, out_keep)
+    g_second_other = hop(g_second, TO_MAIN)
+    out_got = hop(out_send, CORE_SWAP)
+    gs = (own_g, g_other, g_first, g_first_other, g_second_other, g_second)
+    mg, back, ups, hg, sums, hsum = run_upstream(spot, gs, [wd, we, wr, second_row], unit, slope)
+    out_near = near_sum(out_keep, out_got)
+    out_near, hg = tie(out_near, hg)
+    out_got_near = hop(out_near, NEAR_OFF)
+
+    spot = jnp.stack([*spots, col])
+    kept_share, *shares_out = weight_gradients(spot, second, hg, active, ups, mixed)
+    out_home = home_sum(out_keep, out_got, out_near, out_got_near, main)
+    out_home, mg, *shares_out = tie(out_home, mg, *shares_out)
+    out_got_home = hop(out_home, HOME)
+    shares_got = plane(shares_out)
+
+    jb = attend_backward(qkv, mg.reshape(heads, HEAD, total), full, inverse_sum, shares, tables)
+    jb = jb.reshape(-1, total)
+
+    spot = jnp.stack([col, quarter])
+    up_sum = jnp.sum(wide(own_g).reshape(-1, 8, width), axis=0)
+    kept_joint, *joint_out, vector = joint_gradient(
+        spot, jb, unit, wj, first_row, row_of(first_shift), sums, up_sum, hsum
+    )
+    jb, *joint_out = tie(jb, *joint_out)
+    joint_got = plane(joint_out)
+
+    send, keep = deliver(order, jb, wj, back, first_row)
+
+    send, out_got_home, *shares_got = tie(send, out_got_home, *shares_got)
+    got = hop(send, CORE_SWAP)
+    share = wide(kept_share) + sum(wide(piece) for piece in shares_got)
+    kept = near ^ half
+    part = width // 4
+    expand_part = share[:part].reshape(2, 2, 2, part // 8, units // N)
+    reduce_part = share[part : part + units // (4 * N)].reshape(2, -1, width)
+    dense_part = share[part + units // (4 * N) :]
+    far_send = [pick(expand_part, 1, 1 - half).reshape(part // 2, -1), pick(reduce_part, 0, 1 - kept), dense_part]
+    far_send = low(jnp.concatenate(far_send, axis=0))
+    far_got = hop(far_send, FAR_SWAP)
+    near_part = near_sum(keep, got)
+    out = own_sum(out_keep, out_got, out_got_home, main)
+    inputs = wide(own_x)
+    result = low(inputs + out + (dense_bias + reduce_bias))
+    near_part, result = tie(near_part, result)
+    got_near = hop(near_part, NEAR_OFF)
+
+    got_near, *joint_got = tie(got_near, *joint_got)
+    joint_part = wide(kept_joint) + sum(wide(piece[:part]) for piece in joint_got)
+    vector = vector + sum(unpack(piece[part:], width) for piece in joint_got)
+    joint_width = joint_part.shape[1]
+    joint_part = joint_part.reshape(2, 2, 2, part // 8, joint_width)
+    joint_far_send = jnp.concatenate(
+        [low(pick(joint_part, 1, 1 - half)).reshape(part // 2, joint_width), pack(vector, joint_width)], axis=0
+    )
+    far_got = wide(far_got)
+    expand_part = low(pick(expand_part, 1, half).reshape(part // 2, -1) + far_got[: part // 2])
+    reduce_part = low(pick(reduce_part, 0, kept) + far_got[part // 2 : part // 2 + 128])
+    dense_part = low(dense_part + far_got[part // 2 + 128 :]).reshape(2, HEAD // 2, width)
+    home = home_sum(keep, got, near_part, got_near, main)
+    line = jnp.concatenate(
+        [
+            expand_part.reshape(2, 2, part // 8, -1),
+            jnp.broadcast_to(dense_part[None], (2,) + dense_part.shape),
+        ],
+        axis=2,
+    )
+    line_send = first_pieces(line, near)
+    home, joint_far_send, line_send, reduce_part = tie(home, joint_far_send, line_send, reduce_part)
+    line_got = hop(line_send, NEAR)
+    reduce_got = hop(reduce_part, [((c, s), ((s % 2) ^ (s // 2), 2 * (s // 2) + c)) for c, s in PLACES])
+    got_home = hop(home, HOME)
+    joint_far = hop(joint_far_send, FAR_SWAP)
+    line_last = hop(second_pieces(line, line_got, core, near), CORE_SWAP)
+    line_mine = own_pieces(line, line_got, line_last, core, near)
+    expand_got = by_quarter(line_mine, quarter, part // 8)
+    dense_got = pick(jnp.stack([piece[part // 8 :] for piece in line_mine]), 0, 2 * (near ^ core) + (core ^ half))
+    expand_mine = expand_got.reshape(2, 2, -1, groups // 2, 2, 128)
+    expand_mine = jnp.stack([expand_mine[:, :, :, :, 0], expand_mine[::-1, :, :, :, 1]], axis=4)
+    expand_mine = wide(jnp.transpose(expand_mine, (2, 3, 4, 0, 1, 5)).reshape(-1, units))
+    reduce_mine = wide(reduce_got)
+    dense_mine = wide(dense_got)
+
+    joint_part = low(pick(joint_part, 1, half).reshape(part // 2, joint_width) + wide(joint_far[: part // 2]))
+    vector = vector + unpack(joint_far[part // 2 :], width)
+    scaled = own_sum(keep, got, got_home, main)
+    _, unit_rows, inverse_root = normalize(inputs, first_gain, first_shift)
+    input_back = inverse_root * (
+        scaled
+        - jnp.mean(scaled, axis=-1, keepdims=True)
+        - unit_rows * jnp.mean(scaled * unit_rows, axis=-1, keepdims=True)
+    )
+    tokens_gradient = low(wide(own_g) + input_back)
+    joint_part, vector, expand_mine, reduce_mine, dense_mine, tokens_gradient = tie(
+        joint_part, vector, expand_mine, reduce_mine, dense_mine, tokens_gradient
+    )
+    line = joint_part.reshape(2, 2, part // 8, joint_width)
+    line_got = hop(jnp.concatenate([first_pieces(line, near), pack(vector, joint_width)], axis=0), NEAR)
+    vector = vector + unpack(line_got[part // 4 :], width)
+    line_got = line_got[: part // 4]
+    line_last = hop(
+        jnp.concatenate([second_pieces(line, line_got, core, near), pack(vector, joint_width)], axis=0), CORE_SWAP
+    )
+    vector = vector + unpack(line_last[part // 4 :], width)
+    joint_mine = by_quarter(own_pieces(line, line_got, line_last[: part // 4], core, near), quarter, part // 8)
+    joint_mine = joint_mine.reshape(N, -1, 3, heads, HEAD)
+    joint_mine = wide(jnp.transpose(joint_mine, (1, 2, 3, 0, 4)).reshape(-1, 3 * width))
+
+    device = (2 * col + core) * N + z
+    share = width // (8 * N)
+    head_row = lambda head: 5 + N + head % N
+    cut = lambda row, start, size: lax.dynamic_slice(vector, (row, start), (1, size))[0]
+    pieces = [cut(row, device * share, share) for row in range(5)]
+    pieces[4:] = [
+        cut(head_row(device % HEADS), (device // HEADS * heads + device % HEADS // N) * HEAD, HEAD),
+        cut(head_row(device // 2), (2 * heads + device // 2 // N) * HEAD + device % 2 * share, share),
+        pieces[4],
+        cut(5 + (z ^ (2 * core)), (2 * col + core) * 128, 128),
+    ]
+
+    return (
+        result[None],
+        tokens_gradient[None],
+        *pieces[:4],
+        joint_mine,
+        pieces[4],
+        pieces[5],
+        dense_mine,
+        pieces[6],
+        expand_mine,
+        pieces[7],
+        reduce_mine,
+        pieces[6],
+    )
+
+
 def solution(mesh):
-    placed = (
-        P("batch", "blk", None),
-        P("batch", None),
-        P(),
-        P(),
-        P(),
-        P(),
-        P(),
-        P(),
-        P(),
-        P(),
-        P(),
-        P(),
-        P(),
-        P(),
-        P("batch", "blk", None),
-    )
+    count, blocks = mesh.devices.shape
+    split = blocks == N and count == 8
+    if split:
+        mesh = jax.sharding.Mesh(mesh.devices.reshape(count // 2, 2, blocks), ("col", "core", "blk"))
+        batch = ("col", "core")
+        every = ("col", "core", "blk")
+    else:
+        batch, every = "batch", ("batch", "blk")
+    by_rows = P(batch, "blk", None)
+    placed = (by_rows, P(batch, None)) + (P(),) * 12 + (by_rows,)
+    vector, matrix = P(every), P(every, None)
     return jax.shard_map(
-        local,
+        split_local if split else local,
         mesh=mesh,
         in_specs=placed,
         out_specs=(
-            P("batch", "blk", None),
-            P("batch", "blk", None),
-            P(("batch", "blk")),
-            P(("batch", "blk")),
-            P(("batch", "blk")),
-            P(("batch", "blk")),
-            P(("batch", "blk"), None),
-            P(("batch", "blk")),
-            P(("batch", "blk")),
-            P(("batch", "blk"), None),
-            P(("batch", "blk")),
-            P(("batch", "blk"), None),
-            P(("batch", "blk")),
-            P(("batch", "blk"), None),
-            P(("batch", "blk")),
+            by_rows,
+            by_rows,
+            vector,
+            vector,
+            vector,
+            vector,
+            matrix,
+            vector,
+            vector,
+            matrix,
+            vector,
+            matrix,
+            vector,
+            matrix,
+            vector,
         ),
         check_vma=False,
     )

time: 1790 us -> 339 us (0.19)
  waiting for transfers between devices: 1480 us -> 69.1 us
  Pallas kernels: 0 us -> 165 us
  matrix products: 154 us -> 0 us
  starting transfers between devices: 0.67 us -> 46.2 us
  blocking collectives: 42.3 us -> 0 us
  local copies, waits for them, and re-layouts: 61.7 us -> 21 us
    reduce_scatter x5 -> x0, waiting for transfers between devices: 1340 us -> none  [the longest x1 384 us: local(): lax.psum_scatter(back_state[1], 'blk', scatter_dimension=1, tiled=True)]
    pallas_call x0 -> x13, Pallas kernels: none -> 165 us  [the longest x4 41.8 us: run_tokens(): pl.pallas_call(partial(token_kernel, len(data), sub, chunk), grid_spec=pl...]
    dot_general x19 -> x0, matrix products: 154 us -> none  [the longest x4 35.7 us: outer(): lax.dot_general(left_rows, right_rows, (((0,), (0,)), ((), ())), preferre...]
    all_gather x1 -> x0, waiting for transfers between devices: 144 us -> none  [local(): lax.all_gather(pair_local, 'blk', axis=1, tiled=True)]
    ppermute x0 -> x30, waiting for transfers between devices: none -> 69.1 us  [the longest x24 67.9 us: hop(): lax.ppermute(value, ('core', 'blk'), [(a[0] * N + a[1], b[0] * N + b[1])...]
    ppermute x0 -> x30, starting transfers between devices: none -> 46.2 us  [the longest x24 39.1 us: hop(): lax.ppermute(value, ('core', 'blk'), [(a[0] * N + a[1], b[0] * N + b[1])...]
    unnamed x1 -> x0, blocking collectives: 42.3 us -> none
    slice x14 -> x12, local copies, waits for them, and re-layouts: 20.8 us -> 2.7 us  [the longest x1 1.07 us: split_local(): expand_mine[:, :, :, :, 0]]
  transfers between devices with their start and end apart: 6 -> 30, of which waited for: 6 -> 5; matrix products, arithmetic and copies ran while one was open for 7% -> 9% of each run, Pallas kernels for 0% -> 50%
where the time goes in v1:
time: 339 us; the launch traced here: 332 us
  Pallas kernels  165 us (49%)
  waiting for transfers between devices  69.1 us (20%)
  starting transfers between devices  46.2 us (14%)
  other arithmetic  28.6 us (8%)
  local copies, waits for them, and re-layouts  21 us (6%)
    ppermute x24, waiting for transfers between devices, hop(): lax.ppermute(value, ('core', 'blk'), [(a[0] * N + a[1], b[0] * N + b[1])...  67.9 us
    pallas_call x4, Pallas kernels, run_tokens(): pl.pallas_call(partial(token_kernel, len(data), sub, chunk), grid_spec=pl...  41.8 us
    ppermute x24, starting transfers between devices, hop(): lax.ppermute(value, ('core', 'blk'), [(a[0] * N + a[1], b[0] * N + b[1])...  39.1 us
    pallas_call x1, Pallas kernels, attend_backward(): pl.pallas_call(backward_kernel, grid=(heads,), in_specs=[kinds, head_rows...  26.4 us
    pallas_call x2, Pallas kernels, attend_forward(): pl.pallas_call(partial(forward_kernel, len(aliases)), grid=(count,), in_s...  23.7 us
    pallas_call x1, Pallas kernels, run_upstream(): pl.pallas_call(partial(upstream_kernel, chunk), grid_spec=pltpu.PrefetchS...  18.6 us
    pallas_call x1, Pallas kernels, weight_gradients(): pl.pallas_call(weight_kernel, grid_spec=pltpu.PrefetchScalarGridSpec(num_...  16.9 us
    pallas_call x2, Pallas kernels, deliver(): pl.pallas_call(deliver_kernel, grid_spec=pltpu.PrefetchScalarGridSpec(num...  16.6 us
  transfers between devices with their start and end apart: 30, of which 5 were waited for; matrix products, arithmetic and copies ran while one was open for 9% of the time, Pallas kernels for 50%

profile of v1, /device:TPU:0, one launch (start us, length us, event | category | flops | bytes accessed | tf_op | source)
XLA Modules:
  0.0 332.1 jit_solution(5483977595632862468)
XLA Ops:
  0.6 3.3 %collective-permute-start.1 = (bf16[512,1024]{1,0:T(8,128)(2,1)}, bf16[512,1024]{1,0:T(8,128)(2,1)}, u32[]{:S(2)}, u32[]{:S(2)}) collective-permute-start(bf16[512,1024]{1,0:T(8,128)(2,1)} %bitcast.121), channel_id=1, source_target_pairs={{0,4},{1,5},{6,2},{7,3},{8,12},{9,13},{14,10},{15,11},{16,20},{17,... | collective-permute-start | bytes 3145736 | tf_op jit(solution)/shard_map/ppermute | solution.py:990
  4.0 2.4 collective-permute-start
  7.2 1.1 reshape.400.refs_3_.refs_2_
  10.2 10.4 %shard_map.262 = (bf16[768,1024]{1,0:T(8,128)(2,1)}, bf16[256,1024]{1,0:T(8,128)(2,1)}, bf16[1024,1024]{1,0:T(8,128)(2,1)}, bf16[1024,1024]{1,0:T(8,128)(2,1)}) custom-call(s32[1]{0:T(128)} %bitcast.4.spot_ref, bf16[1024,3072]{1,0:T(8,128)(2,1)} %wj_ref.1, bf16[1024,1024]{1,0:T(8,128)(2,1)} %wd_ref.1, bf16[1024,4096]{1,0:T(8,128)(2,1)} %we_ref.1, ...), custom_call_target="tpu_custom_call" | custom-call | bytes 14680064 | tf_op jit(solution)/shard_map/pallas_call | solution.py:392
  22.1 10.6 %shard_map.263 = (bf16[768,2048]{1,0:T(8,128)(2,1)}, bf16[2048,1024]{1,0:T(8,128)(2,1)}, bf16[2048,1024]{1,0:T(8,128)(2,1)}, bf16[2048,1024]{1,0:T(8,128)(2,1)},...) custom-call(s32[2]{0:T(128)} %pad_add_fusion.3.spot_ref, bf16[512,1024]{1,0:T(8,128)(2,1)} %bitcast.123, ...), custom_call_target="tpu_custom_call" | custom-call | flops 5905580032 | bytes 8388608 | tf_op jit(solution)/shard_map/pallas_call | solution.py:668
  34.8 10.3 %shard_map.264 = (bf16[768,2048]{1,0:T(8,128)(2,1)}, bf16[2048,1024]{1,0:T(8,128)(2,1)}, bf16[2048,1024]{1,0:T(8,128)(2,1)}, bf16[2048,1024]{1,0:T(8,128)(2,1)},...) custom-call(s32[2]{0:T(128)} %get-tuple-element.313.spot_ref, ...), custom_call_target="tpu_custom_call", output_to_operand_aliasing={{0}: (13, {}), {1}: (14, {}), {2}: (15, {}), {3}: (16, {}),... | custom-call | flops 5905580032 | bytes 8388608 | tf_op jit(solution)/shard_map/pallas_call | solution.py:668
  45.2 1.5 collective-permute-start.5
  47.3 1.0 select_convert_fusion
  49.1 10.2 %shard_map.265 = (bf16[768,2048]{1,0:T(8,128)(2,1)}, bf16[2048,1024]{1,0:T(8,128)(2,1)}, bf16[2048,1024]{1,0:T(8,128)(2,1)}, bf16[2048,1024]{1,0:T(8,128)(2,1)},...) custom-call(s32[2]{0:T(128)} %get-tuple-element.312.spot_ref, ...), custom_call_target="tpu_custom_call", output_to_operand_aliasing={{0}: (13, {}), {1}: (14, {}), {2}: (15, {}), {3}: (16, {}),... | custom-call | flops 5905580032 | bytes 8388608 | tf_op jit(solution)/shard_map/pallas_call | solution.py:668
  60.3 10.7 %shard_map.266 = (bf16[768,2048]{1,0:T(8,128)(2,1)}, bf16[2048,1024]{1,0:T(8,128)(2,1)}, bf16[2048,1024]{1,0:T(8,128)(2,1)}, bf16[2048,1024]{1,0:T(8,128)(2,1)},...) custom-call(s32[2]{0:T(128)} %pad_add_fusion.2.spot_ref, ...), custom_call_target="tpu_custom_call", output_to_operand_aliasing={{0}: (14, {}), {1}: (15, {}), {2}: (16, {}), {3}: (17, {}),... | custom-call | flops 5905580032 | bytes 8388608 | tf_op jit(solution)/shard_map/pallas_call | solution.py:668
  71.0 12.1 %shard_map.267 = (bf16[4,64,2048]{2,1,0:T(8,128)(2,1)}, f32[4,64,2048]{2,1,0:T(8,128)}, f32[4,1,2048]{2,1,0:T(1,128)}, bf16[4,10,512,512]{3,2,1,0:T(8,128)(2,1)}) custom-call(bf16[3,4,64,2048]{3,2,1,0:T(8,128)(2,1)} %bitcast.118, bf16[64,2048]{1,0:T(8,128)(2,1)} %get-tuple-element.309.kx_ref, bf16[64,2048]{1,0:T(8,128)(2,1)} %get-tuple-element.308.qx_ref), custom_call_target="tpu_custom_call" | custom-call | flops 5368709120 | bytes 10485760 | tf_op jit(solution)/shard_map/pallas_call | solution.py:490
  83.0 1.6 collective-permute-start.7
  85.2 10.0 %collective-permute-start.9 = (bf16[512,1024]{1,0:T(8,128)(2,1)S(1)}, bf16[512,1024]{1,0:T(8,128)(2,1)}, u32[]{:S(2)}, u32[]{:S(2)}) collective-permute-start(bf16[512,1024]{1,0:T(8,128)(2,1)S(1)} %bitcast.128), channel_id=1, source_target_pairs={{0,4},{1,5},{6,2},{7,3},{8,12},{9,13},{14,10},{15,11},{16,20},{17,... | collective-permute-start | bytes 3145736 | tf_op jit(solution)/shard_map/ppermute | solution.py:990
  95.2 11.7 %shard_map.268 = (bf16[4,64,2048]{2,1,0:T(8,128)(2,1)}, f32[4,64,2048]{2,1,0:T(8,128)}, f32[4,1,2048]{2,1,0:T(1,128)}, bf16[4,10,512,512]{3,2,1,0:T(8,128)(2,1)}) custom-call(bf16[3,4,64,2048]{3,2,1,0:T(8,128)(2,1)} %bitcast.119, ...), custom_call_target="tpu_custom_call", output_to_operand_aliasing={{0}: (3, {}), {1}: (4, {}), {2}: (5, {}), {3}: (6, {})} | custom-call | flops 5368709120 | bytes 10485760 | tf_op jit(solution)/shard_map/pallas_call | solution.py:490
  106.9 7.0 %shard_map.269 = (bf16[1024,1024]{1,0:T(8,128)(2,1)}, bf16[1024,1024]{1,0:T(8,128)(2,1)}) custom-call(s32[4]{0:T(128)} %xor_xor_fusion.order_ref, bf16[256,2048]{1,0:T(8,128)(2,1)} %bitcast.129, bf16[256,1024]{1,0:T(8,128)(2,1)} %get-tuple-element.177.weight_ref.refs_6_, bf16[2048,1024]{1,0:T(8,128)(2,1)} %get-tuple-element.178.add_ref), custom_call_target="tpu_custom_call" | custom-call | tf_op jit(solution)/shard_map/pallas_call | solution.py:866
  113.9 1.3 collective-permute-start.11
  115.8 2.1 collective-permute-start.8
  119.9 18.6 %shard_map.270 = (bf16[256,2048]{1,0:T(8,128)(2,1)}, bf16[2048,1024]{1,0:T(8,128)(2,1)}, bf16[2048,1024]{1,0:T(8,128)(2,1)}, bf16[2048,1024]{1,0:T(8,128)(2,1)},...) custom-call(s32[8]{0:T(128)} %stack.118.spot_ref, bf16[512,1024]{1,0:T(8,128)(2,1)} %bitcast.126, ...), custom_call_target="tpu_custom_call" | custom-call | flops 14495514624 | bytes 25165824 | tf_op jit(solution)/shard_map/pallas_call | solution.py:750
  139.6 16.9 %shard_map.271 = (bf16[576,1024]{1,0:T(8,128)(2,1)}, bf16[576,1024]{1,0:T(8,128)(2,1)}, bf16[576,1024]{1,0:T(8,128)(2,1)}, bf16[576,1024]{1,0:T(8,128)(2,1)}) custom-call(s32[5]{0:T(128)} %stack.120.spot_ref, bf16[2048,1024]{1,0:T(8,128)(2,1)} %get-tuple-element.192.second_ref, bf16[2048,1024]{1,0:T(8,128)(2,1)} %get-tuple-element.193.hg_ref, ...), custom_call_target="tpu_custom_call" | custom-call | flops 14495514624 | bytes 16777216 | tf_op jit(solution)/shard_map/pallas_call | solution.py:806
  157.4 1.6 collective-permute-start.14
  159.0 1.5 collective-permute-start.15
  161.0 1.6 collective-permute-start.13
  162.6 26.4 %shard_map.272 = bf16[3,4,64,2048]{3,2,1,0:T(8,128)(2,1)} custom-call(bf16[3,4,64,2048]{3,2,1,0:T(8,128)(2,1)} %bitcast.120, bf16[4,64,2048]{2,1,0:T(8,128)(2,1)} %bitcast.180, f32[4,64,2048]{2,1,0:T(8,128)} %get-tuple-element.200.full_ref, f32[4,1,2048]{2,1,0:T(1,128)} %get-tuple-element.201.inverse_ref, ...), custom_call_target="tpu_custom_call" | custom-call | flops 21474836480 | bytes 20971520 | tf_op jit(solution)/shard_map/pallas_call | solution.py:571
  189.0 10.7 %shard_map.273 = (bf16[256,768]{1,0:T(8,128)(2,1)}, bf16[320,768]{1,0:T(8,128)(2,1)}, bf16[320,768]{1,0:T(8,128)(2,1)}, bf16[320,768]{1,0:T(8,128)(2,1)}, f32[16,1024]{1,0:T(8,128)}) custom-call(s32[2]{0:T(128)} %pad_add_fusion.4.spot_ref, bf16[768,2048]{1,0:T(8,128)(2,1)} %bitcast.124, bf16[2048,1024]{1,0:T(8,128)(2,1)} %get-tuple-element.187.refs_10_.unit_ref, ...), custom_call_target="tpu_custom_call" | custom-call | tf_op jit(solution)/shard_map/pallas_call | solution.py:944
  199.7 9.6 %shard_map.274 = (bf16[1024,1024]{1,0:T(8,128)(2,1)}, bf16[1024,1024]{1,0:T(8,128)(2,1)}) custom-call(s32[4]{0:T(128)} %xor_xor_fusion.order_ref, bf16[768,2048]{1,0:T(8,128)(2,1)} %bitcast.125, bf16[768,1024]{1,0:T(8,128)(2,1)} %get-tuple-element.129.refs_2_.refs_1_.wj_ref.weight_ref, bf16[2048,1024]{1,0:T(8,128)(2,1)} %get-tuple-element.209.add_ref, ...), custom_call_target="tpu_custom_call" | custom-call | tf_op jit(solution)/shard_map/pallas_call | solution.py:866
  210.3 1.2 collective-permute-done.16
  211.5 1.8 collective-permute-start.17
  214.5 1.1 collective-permute-start.20
  215.6 1.4 collective-permute-start.21
  217.1 2.6 add_add_fusion
  220.2 1.1 copy-done.5
  222.3 1.9 fusion.9
  224.2 1.6 add_convert_fusion.1
  226.6 24.5 %collective-permute-done.22 = bf16[320,1024]{1,0:T(8,128)(2,1)S(1)} collective-permute-done((bf16[320,1024]{1,0:T(8,128)(2,1)S(1)}, bf16[320,1024]{1,0:T(8,128)(2,1)S(1)}, u32[]{:S(2)}, u32[]{:S(2)}) %collective-permute-start.22) | collective-permute-done | bytes 655392 | tf_op jit(solution)/shard_map/ppermute | solution.py:990
  252.8 3.1 fusion.13
  256.7 4.4 %collective-permute-start.27 = (bf16[512,1024]{1,0:T(8,128)(2,1)}, bf16[512,1024]{1,0:T(8,128)(2,1)}, u32[]{:S(2)}, u32[]{:S(2)}) collective-permute-start(bf16[512,1024]{1,0:T(8,128)(2,1)} %fusion.13), channel_id=1, source_target_pairs={{0,1},{1,0},{6,7},{7,6},{2,4},{3,5},{4,2},{5,3},{8,9},{9,8},{14,15... | collective-permute-start | bytes 3145736 | tf_op jit(solution)/shard_map/ppermute | solution.py:990
  261.1 4.2 %collective-permute-start.23 = (bf16[192,768]{1,0:T(8,128)(2,1)S(1)}, bf16[192,768]{1,0:T(8,128)(2,1)S(1)}, u32[]{:S(2)}, u32[]{:S(2)}) collective-permute-start(bf16[192,768]{1,0:T(8,128)(2,1)S(1)} %constant_dynamic-update-slice_fusion), channel_id=1, source_target_pairs={{0,2},{1,3},{2,0},{3,1},{4,6},{5,7},{6,4},{7,5},{8,10},{9,11},{10,... | collective-permute-start | bytes 884744 | tf_op jit(solution)/shard_map/ppermute | solution.py:990
  266.9 35.2 %collective-permute-done.23 = bf16[192,768]{1,0:T(8,128)(2,1)S(1)} collective-permute-done((bf16[192,768]{1,0:T(8,128)(2,1)S(1)}, bf16[192,768]{1,0:T(8,128)(2,1)S(1)}, u32[]{:S(2)}, u32[]{:S(2)}) %collective-permute-start.23) | collective-permute-done | bytes 294944 | tf_op jit(solution)/shard_map/ppermute | solution.py:990
  304.4 1.1 reshape.391
  305.5 1.1 fusion.41
  306.9 1.2 copy.85
  308.0 1.1 convert_bitcast_fusion
  309.1 2.3 reshape.396
  312.1 2.6 fusion.38
  314.7 3.6 %fusion.8 = bf16[512,1024]{1,0:T(8,128)(2,1)} fusion(f32[512]{0:T(512)S(1)} %broadcast_multiply_fusion, f32[512]{0:T(512)S(1)} %broadcast_multiply_fusion.1, f32[512]{0:T(512)S(1)} %add_rsqrt_fusion, f32[512]{0:T(512)S(1)} %broadcast_multiply_fusion.2, bf16[1,512,1024]{2,1,0:T(8,128)(2,1)S(1)} %copy-done.7, bf16[1,512,1024]{2,1,0:T(8,128)(2,1)S(1)} %copy-done, ...), kind=kLoop, calls=%fused_computation.12 | loop fusion | flops 8388608 | bytes 6299649 | tf_op jit(solution)/shard_map/convert_element_type | solution.py:344
  318.6 6.8 %collective-permute-done.28 = bf16[128,768]{1,0:T(8,128)(2,1)S(1)} collective-permute-done((bf16[128,768]{1,0:T(8,128)(2,1)S(1)}, bf16[128,768]{1,0:T(8,128)(2,1)S(1)}, u32[]{:S(2)}, u32[]{:S(2)}) %collective-permute-start.28) | collective-permute-done | bytes 196640 | tf_op jit(solution)/shard_map/ppermute | solution.py:990
  325.7 1.4 collective-permute-done.29
  328.1 1.3 reshape.398
  (197 shorter events, 29.5 us)
Async XLA Ops:
  0.6 21.5 %collective-permute-start.1 = (bf16[512,1024]{1,0:T(8,128)(2,1)}, bf16[512,1024]{1,0:T(8,128)(2,1)}, u32[]{:S(2)}, u32[]{:S(2)}) collective-permute-start(bf16[512,1024]{1,0:T(8,128)(2,1)} %bitcast.121), channel_id=1, source_target_pairs={{0,4},{1,5},{6,2},{7,3},{8,12},{9,13},{14,10},{15,11},{16,20},{17,... | collective-permute-start | bytes 3145736 | tf_op jit(solution)/shard_map/ppermute | solution.py:990
  4.0 28.7 %collective-permute-start = (bf16[512,1024]{1,0:T(8,128)(2,1)}, bf16[512,1024]{1,0:T(8,128)(2,1)S(1)}, u32[]{:S(2)}, u32[]{:S(2)}) collective-permute-start(bf16[512,1024]{1,0:T(8,128)(2,1)} %bitcast.122), channel_id=1, source_target_pairs={{0,1},{1,0},{6,7},{7,6},{2,4},{3,5},{4,2},{5,3},{8,9},{9,8},{14,15... | collective-permute-start | bytes 3145736 | tf_op jit(solution)/shard_map/ppermute | solution.py:990
  6.4 14.3 %collective-permute-start.2 = (s32[1,4]{1,0:T(1,128)}, s32[1,4]{1,0:T(1,128)S(1)}, u32[]{:S(2)}, u32[]{:S(2)}) collective-permute-start(s32[1,4]{1,0:T(1,128)} %param.16), channel_id=1, source_target_pairs={{0,4},{1,5},{2,6},{3,7},{4,0},{5,1},{6,2},{7,3},{8,12},{9,13},{10,... | collective-permute-start | bytes 56 | tf_op jit(solution)/shard_map/ppermute | solution.py:990
  10.2 10.5 %copy-start.19 = (s32[1,4]{1,0:T(1,128)S(1)}, s32[1,4]{1,0:T(1,128)}, u32[]{:S(2)}) copy-start(s32[1,4]{1,0:T(1,128)} %param.16) | copy-start | bytes 52
  32.7 2.1 copy-start.9
  32.7 12.4 %collective-permute-start.3 = (bf16[512,1024]{1,0:T(8,128)(2,1)S(1)}, bf16[512,1024]{1,0:T(8,128)(2,1)}, u32[]{:S(2)}, u32[]{:S(2)}) collective-permute-start(bf16[512,1024]{1,0:T(8,128)(2,1)S(1)} %collective-permute-done.refs_0_), channel_id=1, source_target_pairs={{0,4},{1,5},{2,6},{3,7},{4,0},{5,1},{6,2},{7,3},{8,12},{9,13},{10,... | collective-permute-start | bytes 3145736 | tf_op jit(solution)/shard_map/ppermute | solution.py:990
  33.3 11.8 %collective-permute-start.4 = (bf16[512,1024]{1,0:T(8,128)(2,1)S(1)}, bf16[512,1024]{1,0:T(8,128)(2,1)S(1)}, u32[]{:S(2)}, u32[]{:S(2)}) collective-permute-start(bf16[512,1024]{1,0:T(8,128)(2,1)S(1)} %collective-permute-done.refs_0_), channel_id=1, source_target_pairs={{2,3},{3,2},{4,5},{5,4},{10,11},{11,10},{12,13},{13,12},{18,19},{1... | collective-permute-start | bytes 3145736 | tf_op jit(solution)/shard_map/ppermute | solution.py:990
  34.8 13.4 %copy-start.6 = (bf16[1,512,1024]{2,1,0:T(8,128)(2,1)S(1)}, bf16[1,512,1024]{2,1,0:T(8,128)(2,1)}, u32[]{:S(2)}) copy-start(bf16[1,512,1024]{2,1,0:T(8,128)(2,1)} %param.29) | copy-start | bytes 3145732
  45.2 14.2 %copy-start.10 = (bf16[512,1024]{1,0:T(8,128)(2,1)}, bf16[512,1024]{1,0:T(8,128)(2,1)S(1)}, u32[]{:S(2)}) copy-start(bf16[512,1024]{1,0:T(8,128)(2,1)S(1)} %collective-permute-done.4.refs_1_) | copy-start | bytes 3145732
  45.2 14.1 %collective-permute-start.5 = (bf16[512,1024]{1,0:T(8,128)(2,1)S(1)}, bf16[512,1024]{1,0:T(8,128)(2,1)S(1)}, u32[]{:S(2)}, u32[]{:S(2)}) collective-permute-start(bf16[512,1024]{1,0:T(8,128)(2,1)S(1)} %collective-permute-done.4.refs_1_), channel_id=1, source_target_pairs={{2,6},{3,7},{4,0},{5,1},{10,14},{11,15},{12,8},{13,9},{18,22},{19,... | collective-permute-start | bytes 3145736 | tf_op jit(solution)/shard_map/ppermute | solution.py:990
  48.3 34.8 %collective-permute-start.6 = (bf16[512,1024]{1,0:T(8,128)(2,1)S(1)}, bf16[512,1024]{1,0:T(8,128)(2,1)}, u32[]{:S(2)}, u32[]{:S(2)}) collective-permute-start(bf16[512,1024]{1,0:T(8,128)(2,1)S(1)} %bitcast.127), channel_id=1, source_target_pairs={{0,1},{1,0},{6,7},{7,6},{2,4},{3,5},{4,2},{5,3},{8,9},{9,8},{14,15... | collective-permute-start | bytes 3145736 | tf_op jit(solution)/shard_map/ppermute | solution.py:990
  83.0 30.9 %collective-permute-start.7 = (bf16[512,1024]{1,0:T(8,128)(2,1)}, bf16[512,1024]{1,0:T(8,128)(2,1)}, u32[]{:S(2)}, u32[]{:S(2)}) collective-permute-start(bf16[512,1024]{1,0:T(8,128)(2,1)} %collective-permute-done.6.refs_2_), channel_id=1, source_target_pairs={{2,3},{3,2},{4,5},{5,4},{10,11},{11,10},{12,13},{13,12},{18,19},{1... | collective-permute-start | bytes 3145736 | tf_op jit(solution)/shard_map/ppermute | solution.py:990
  85.2 34.7 %collective-permute-start.9 = (bf16[512,1024]{1,0:T(8,128)(2,1)S(1)}, bf16[512,1024]{1,0:T(8,128)(2,1)}, u32[]{:S(2)}, u32[]{:S(2)}) collective-permute-start(bf16[512,1024]{1,0:T(8,128)(2,1)S(1)} %bitcast.128), channel_id=1, source_target_pairs={{0,4},{1,5},{6,2},{7,3},{8,12},{9,13},{14,10},{15,11},{16,20},{17,... | collective-permute-start | bytes 3145736 | tf_op jit(solution)/shard_map/ppermute | solution.py:990
  95.2 24.7 %collective-permute-start.10 = (bf16[512,1024]{1,0:T(8,128)(2,1)}, bf16[512,1024]{1,0:T(8,128)(2,1)}, u32[]{:S(2)}, u32[]{:S(2)}) collective-permute-start(bf16[512,1024]{1,0:T(8,128)(2,1)} %collective-permute-done.6.refs_2_), channel_id=1, source_target_pairs={{0,4},{1,5},{2,6},{3,7},{4,0},{5,1},{6,2},{7,3},{8,12},{9,13},{10,... | collective-permute-start | bytes 3145736 | tf_op jit(solution)/shard_map/ppermute | solution.py:990
  113.9 6.0 %collective-permute-start.11 = (bf16[512,1024]{1,0:T(8,128)(2,1)}, bf16[512,1024]{1,0:T(8,128)(2,1)}, u32[]{:S(2)}, u32[]{:S(2)}) collective-permute-start(bf16[512,1024]{1,0:T(8,128)(2,1)} %collective-permute-done.7.refs_5_), channel_id=1, source_target_pairs={{2,6},{3,7},{4,0},{5,1},{10,14},{11,15},{12,8},{13,9},{18,22},{19,... | collective-permute-start | bytes 3145736 | tf_op jit(solution)/shard_map/ppermute | solution.py:990
  115.8 22.6 %collective-permute-start.8 = (bf16[1024,1024]{1,0:T(8,128)(2,1)}, bf16[1024,1024]{1,0:T(8,128)(2,1)S(1)}, u32[]{:S(2)}, u32[]{:S(2)}) collective-permute-start(bf16[1024,1024]{1,0:T(8,128)(2,1)} %get-tuple-element.184), channel_id=1, source_target_pairs={{0,4},{1,5},{2,6},{3,7},{4,0},{5,1},{6,2},{7,3},{8,12},{9,13},{10,... | collective-permute-start | bytes 6291464 | tf_op jit(solution)/shard_map/ppermute | solution.py:990
  119.9 18.6 %copy-start.2 = (bf16[1024,1024]{1,0:T(8,128)(2,1)S(1)}, bf16[1024,1024]{1,0:T(8,128)(2,1)}, u32[]{:S(2)}) copy-start(bf16[1024,1024]{1,0:T(8,128)(2,1)} %get-tuple-element.183) | copy-start | bytes 6291460
  138.5 18.1 %copy-start.4 = (bf16[1024,1024]{1,0:T(8,128)(2,1)}, bf16[1024,1024]{1,0:T(8,128)(2,1)S(1)}, u32[]{:S(2)}) copy-start(bf16[1024,1024]{1,0:T(8,128)(2,1)S(1)} %collective-permute-done.8) | copy-start | bytes 6291460
  138.9 17.6 %collective-permute-start.12 = (bf16[512,1024]{1,0:T(8,128)(2,1)S(1)}, bf16[512,1024]{1,0:T(8,128)(2,1)S(1)}, u32[]{:S(2)}, u32[]{:S(2)}) collective-permute-start(bf16[512,1024]{1,0:T(8,128)(2,1)S(1)} %add_convert_fusion.3), channel_id=1, source_target_pairs={{2,3},{3,2},{4,5},{5,4},{10,11},{11,10},{12,13},{13,12},{18,19},{1... | collective-permute-start | bytes 3145736 | tf_op jit(solution)/shard_map/ppermute | solution.py:990
  157.4 51.9 %collective-permute-start.14 = (bf16[576,1024]{1,0:T(8,128)(2,1)}, bf16[576,1024]{1,0:T(8,128)(2,1)S(1)}, u32[]{:S(2)}, u32[]{:S(2)}) collective-permute-start(bf16[576,1024]{1,0:T(8,128)(2,1)} %get-tuple-element.213), channel_id=1, source_target_pairs={{0,8},{8,0},{16,24},{24,16},{1,9},{9,1},{17,25},{25,17},{2,10},{10... | collective-permute-start | bytes 3538952 | tf_op jit(solution)/shard_map/ppermute | solution.py:1032
  159.0 51.3 %collective-permute-start.15 = (bf16[576,1024]{1,0:T(8,128)(2,1)}, bf16[576,1024]{1,0:T(8,128)(2,1)}, u32[]{:S(2)}, u32[]{:S(2)}) collective-permute-start(bf16[576,1024]{1,0:T(8,128)(2,1)} %get-tuple-element.214), channel_id=1, source_target_pairs={{0,16},{8,24},{16,0},{24,8},{1,17},{9,25},{17,1},{25,9},{2,18},{10... | collective-permute-start | bytes 3538952 | tf_op jit(solution)/shard_map/ppermute | solution.py:1032
  160.5 50.9 %collective-permute-start.16 = (bf16[576,1024]{1,0:T(8,128)(2,1)}, bf16[576,1024]{1,0:T(8,128)(2,1)}, u32[]{:S(2)}, u32[]{:S(2)}) collective-permute-start(bf16[576,1024]{1,0:T(8,128)(2,1)} %get-tuple-element.215), channel_id=1, source_target_pairs={{0,24},{8,16},{16,8},{24,0},{1,25},{9,17},{17,9},{25,1},{2,26},{10... | collective-permute-start | bytes 3538952 | tf_op jit(solution)/shard_map/ppermute | solution.py:1032
  161.0 48.3 %collective-permute-start.13 = (bf16[512,1024]{1,0:T(8,128)(2,1)S(1)}, bf16[512,1024]{1,0:T(8,128)(2,1)S(1)}, u32[]{:S(2)}, u32[]{:S(2)}) collective-permute-start(bf16[512,1024]{1,0:T(8,128)(2,1)S(1)} %fusion.12), channel_id=1, source_target_pairs={{0,1},{1,0},{6,7},{7,6},{2,4},{3,5},{4,2},{5,3},{8,9},{9,8},{14,15... | collective-permute-start | bytes 3145736 | tf_op jit(solution)/shard_map/ppermute | solution.py:990
  199.7 13.6 %copy-start.17 = (f32[1024]{0:T(1024)S(1)}, f32[1024]{0:T(1024)}, u32[]{:S(2)}) copy-start(f32[1024]{0:T(1024)} %param.24) | copy-start | bytes 12292
  199.7 13.6 %copy-start.18 = (f32[1024]{0:T(1024)S(1)}, f32[1024]{0:T(1024)}, u32[]{:S(2)}) copy-start(f32[1024]{0:T(1024)} %param.28) | copy-start | bytes 12292
  199.7 13.6 %copy-start = (bf16[1,512,1024]{2,1,0:T(8,128)(2,1)S(1)}, bf16[1,512,1024]{2,1,0:T(8,128)(2,1)}, u32[]{:S(2)}) copy-start(bf16[1,512,1024]{2,1,0:T(8,128)(2,1)} %param.15) | copy-start | bytes 3145732
  199.7 17.4 %copy-start.8 = (bf16[576,1024]{1,0:T(8,128)(2,1)S(1)}, bf16[576,1024]{1,0:T(8,128)(2,1)}, u32[]{:S(2)}) copy-start(bf16[576,1024]{1,0:T(8,128)(2,1)} %get-tuple-element.229) | copy-start | bytes 3538948
  211.5 12.7 %collective-permute-start.17 = (bf16[1024,1024]{1,0:T(8,128)(2,1)}, bf16[1024,1024]{1,0:T(8,128)(2,1)}, u32[]{:S(2)}, u32[]{:S(2)}) collective-permute-start(bf16[1024,1024]{1,0:T(8,128)(2,1)} %get-tuple-element.216), channel_id=1, source_target_pairs={{0,4},{1,5},{2,6},{3,7},{4,0},{5,1},{6,2},{7,3},{8,12},{9,13},{10,... | collective-permute-start | bytes 6291464 | tf_op jit(solution)/shard_map/ppermute | solution.py:990
  213.5 38.0 %collective-permute-start.19 = (bf16[320,768]{1,0:T(8,128)(2,1)}, bf16[320,768]{1,0:T(8,128)(2,1)S(1)}, u32[]{:S(2)}, u32[]{:S(2)}) collective-permute-start(bf16[320,768]{1,0:T(8,128)(2,1)} %get-tuple-element.221), channel_id=1, source_target_pairs={{0,8},{8,0},{16,24},{24,16},{1,9},{9,1},{17,25},{25,17},{2,10},{10... | collective-permute-start | bytes 1474568 | tf_op jit(solution)/shard_map/ppermute | solution.py:1032
  214.5 37.0 %collective-permute-start.20 = (bf16[320,768]{1,0:T(8,128)(2,1)}, bf16[320,768]{1,0:T(8,128)(2,1)S(1)}, u32[]{:S(2)}, u32[]{:S(2)}) collective-permute-start(bf16[320,768]{1,0:T(8,128)(2,1)} %get-tuple-element.222), channel_id=1, source_target_pairs={{0,16},{8,24},{16,0},{24,8},{1,17},{9,25},{17,1},{25,9},{2,18},{10... | collective-permute-start | bytes 1474568 | tf_op jit(solution)/shard_map/ppermute | solution.py:1032
  215.6 35.9 %collective-permute-start.21 = (bf16[320,768]{1,0:T(8,128)(2,1)}, bf16[320,768]{1,0:T(8,128)(2,1)S(1)}, u32[]{:S(2)}, u32[]{:S(2)}) collective-permute-start(bf16[320,768]{1,0:T(8,128)(2,1)} %get-tuple-element.223), channel_id=1, source_target_pairs={{0,24},{8,16},{16,8},{24,0},{1,25},{9,17},{17,9},{25,1},{2,26},{10... | collective-permute-start | bytes 1474568 | tf_op jit(solution)/shard_map/ppermute | solution.py:1032
  219.7 1.6 copy-start.5
  219.7 1.8 copy-start.13
  220.0 2.3 copy-start.3
  220.1 4.1 %copy-start.1 = (bf16[1024,1024]{1,0:T(8,128)(2,1)S(1)}, bf16[1024,1024]{1,0:T(8,128)(2,1)}, u32[]{:S(2)}) copy-start(bf16[1024,1024]{1,0:T(8,128)(2,1)} %get-tuple-element.210) | copy-start | bytes 6291460
  220.1 30.9 %collective-permute-start.22 = (bf16[320,1024]{1,0:T(8,128)(2,1)S(1)}, bf16[320,1024]{1,0:T(8,128)(2,1)S(1)}, u32[]{:S(2)}, u32[]{:S(2)}) collective-permute-start(bf16[320,1024]{1,0:T(8,128)(2,1)S(1)} %pad_maximum_fusion), channel_id=1, source_target_pairs={{0,2},{1,3},{2,0},{3,1},{4,6},{5,7},{6,4},{7,5},{8,10},{9,11},{10,... | collective-permute-start | bytes 1966088 | tf_op jit(solution)/shard_map/ppermute | solution.py:990
  225.8 25.8 %collective-permute-start.18 = (bf16[512,1024]{1,0:T(8,128)(2,1)S(1)}, bf16[512,1024]{1,0:T(8,128)(2,1)S(1)}, u32[]{:S(2)}, u32[]{:S(2)}) collective-permute-start(bf16[512,1024]{1,0:T(8,128)(2,1)S(1)} %add_convert_fusion.1), channel_id=1, source_target_pairs={{2,3},{3,2},{4,5},{5,4},{10,11},{11,10},{12,13},{13,12},{18,19},{1... | collective-permute-start | bytes 3145736 | tf_op jit(solution)/shard_map/ppermute | solution.py:990
  251.7 1.1 copy-start.16
  255.9 9.3 %collective-permute-start.24 = (bf16[128,1024]{1,0:T(8,128)(2,1)S(1)}, bf16[128,1024]{1,0:T(8,128)(2,1)S(1)}, u32[]{:S(2)}, u32[]{:S(2)}) collective-permute-start(bf16[128,1024]{1,0:T(8,128)(2,1)S(1)} %bitcast.153), channel_id=1, source_target_pairs={{0,1},{1,0},{2,3},{3,2},{4,5},{5,4},{6,7},{7,6},{8,9},{9,8},{10,11... | collective-permute-start | bytes 786440 | tf_op jit(solution)/shard_map/ppermute | solution.py:990
  256.0 9.5 %collective-permute-start.26 = (bf16[128,1024]{1,0:T(8,128)(2,1)S(1)}, bf16[128,1024]{1,0:T(8,128)(2,1)S(1)}, u32[]{:S(2)}, u32[]{:S(2)}) collective-permute-start(bf16[128,1024]{1,0:T(8,128)(2,1)S(1)} %get-tuple-element.235), channel_id=1, source_target_pairs={{0,0},{1,4},{2,6},{3,2},{4,1},{5,5},{6,7},{7,3},{8,8},{9,12},{10,1... | collective-permute-start | bytes 786440 | tf_op jit(solution)/shard_map/ppermute | solution.py:990
  256.7 55.4 %collective-permute-start.27 = (bf16[512,1024]{1,0:T(8,128)(2,1)}, bf16[512,1024]{1,0:T(8,128)(2,1)}, u32[]{:S(2)}, u32[]{:S(2)}) collective-permute-start(bf16[512,1024]{1,0:T(8,128)(2,1)} %fusion.13), channel_id=1, source_target_pairs={{0,1},{1,0},{6,7},{7,6},{2,4},{3,5},{4,2},{5,3},{8,9},{9,8},{14,15... | collective-permute-start | bytes 3145736 | tf_op jit(solution)/shard_map/ppermute | solution.py:990
  261.1 41.0 %collective-permute-start.23 = (bf16[192,768]{1,0:T(8,128)(2,1)S(1)}, bf16[192,768]{1,0:T(8,128)(2,1)S(1)}, u32[]{:S(2)}, u32[]{:S(2)}) collective-permute-start(bf16[192,768]{1,0:T(8,128)(2,1)S(1)} %constant_dynamic-update-slice_fusion), channel_id=1, source_target_pairs={{0,2},{1,3},{2,0},{3,1},{4,6},{5,7},{6,4},{7,5},{8,10},{9,11},{10,... | collective-permute-start | bytes 884744 | tf_op jit(solution)/shard_map/ppermute | solution.py:990
  265.3 37.6 %collective-permute-start.25 = (bf16[128,1024]{1,0:T(8,128)(2,1)S(1)}, bf16[128,1024]{1,0:T(8,128)(2,1)S(1)}, u32[]{:S(2)}, u32[]{:S(2)}) collective-permute-start(bf16[128,1024]{1,0:T(8,128)(2,1)S(1)} %pad_maximum_fusion.1), channel_id=1, source_target_pairs={{0,4},{1,5},{2,6},{3,7},{4,0},{5,1},{6,2},{7,3},{8,12},{9,13},{10,... | collective-permute-start | bytes 786440 | tf_op jit(solution)/shard_map/ppermute | solution.py:990
  312.1 2.6 copy-start.7
  314.7 3.6 %copy-start.14 = (bf16[128,768]{1,0:T(8,128)(2,1)S(1)}, bf16[128,768]{1,0:T(8,128)(2,1)}, u32[]{:S(2)}) copy-start(bf16[128,768]{1,0:T(8,128)(2,1)} %fusion.19) | copy-start | bytes 589828
  318.4 7.1 %collective-permute-start.28 = (bf16[128,768]{1,0:T(8,128)(2,1)S(1)}, bf16[128,768]{1,0:T(8,128)(2,1)S(1)}, u32[]{:S(2)}, u32[]{:S(2)}) collective-permute-start(bf16[128,768]{1,0:T(8,128)(2,1)S(1)} %constant_dynamic-update-slice_fusion.5), channel_id=1, source_target_pairs={{0,1},{1,0},{2,3},{3,2},{4,5},{5,4},{6,7},{7,6},{8,9},{9,8},{10,11... | collective-permute-start | bytes 589832 | tf_op jit(solution)/shard_map/ppermute | solution.py:990
  325.6 1.5 collective-permute-start.29
  330.1 1.7 copy-start.20
  (3 other events, 2.9 us)

commit v2 on v1

--- a/solution.py
+++ b/solution.py
@@ -595,18 +595,24 @@
     )(qkv, mg, full, inverse, shares, *tables)
 
 
+def chosen(index, options):
+    value = options[-1]
+    for k in reversed(range(len(options) - 1)):
+        value = jnp.where(index == k, options[k], value)
+    return value
+
+
 def token_kernel(count, sub, chunk, spot_ref, *refs):
-    a_ref, b_ref = refs[0], refs[count - 1]
+    sources = refs[:count]
     (wj_ref, bj_ref, we_ref, be_ref, wr_ref, g1_ref, s1_ref, g2_ref, s2_ref, cos_ref, sin_ref) = refs[count : count + 11]
     qkv_ref, unit_ref, second_ref, active_ref, slope_ref, feed_ref = refs[-6:]
-    step = pl.program_id(0)
-    pick_b = spot_ref[pl.num_programs(0) + step] == 1
-    rows = a_ref.shape[0]
+    choice = spot_ref[pl.num_programs(0) + pl.program_id(0)]
+    rows = sources[0].shape[0]
     half = ROTARY // 2
     part = wj_ref.shape[0] // 3
     for top in range(0, rows, sub):
         at = slice(top, top + sub)
-        x = wide(a_ref[at, :] if count == 1 else jnp.where(pick_b, b_ref[at, :], a_ref[at, :]))
+        x = wide(chosen(choice, [source[at, :] for source in sources]))
         center = x - jnp.mean(x, axis=-1, keepdims=True)
         scale = lax.rsqrt(jnp.mean(center * center, axis=-1, keepdims=True) + EPSILON)
         unit = center * scale
@@ -639,8 +645,8 @@
         feed_ref[at, :] = low(mm(active_ref[at, :], wr_ref[...]))
 
 
-def run_tokens(slot, spot, a, b, weights, tables, before, sub=256, chunk=256):
-    rows, width = a.shape
+def run_tokens(slot, spot, data, weights, tables, before, sub=256, chunk=256):
+    rows, width = data[0].shape
     total = tables[0].shape[1]
     wj, bj, we, be, wr, g1, s1, g2, s2 = weights
     units = we.shape[1]
@@ -652,7 +658,6 @@
     column = lambda height: pl.BlockSpec((height, rows), lambda i, spot: (0, spot[i]))
     placed = pl.BlockSpec((rows, width), lambda i, spot: (spot[i], 0))
     arrived = lambda size: pl.BlockSpec((rows, size), lambda i, spot: (slot + i, 0))
-    data = [a] if a is b else [a, b]
     in_specs = [whole(w) for w in (*data, *weights)] + [column(ROTARY // 2)] * 2
     out_specs = [column(wj.shape[0]), placed, arrived(width), arrived(units), arrived(units), placed]
     shape = lambda *dims: jax.ShapeDtypeStruct(dims, jnp.bfloat16)
@@ -664,7 +669,6 @@
             aliases[len(operands)] = index
             operands.append(array)
             in_specs.append(pl.BlockSpec(memory_space=pl.ANY))
-    products = steps * rows * width * (wj.shape[0] + 2 * units)
     return pl.pallas_call(
         partial(token_kernel, len(data), sub, chunk),
         grid_spec=pltpu.PrefetchScalarGridSpec(
@@ -673,9 +677,7 @@
         out_shape=out_shape,
         input_output_aliases=aliases,
         compiler_params=pltpu.CompilerParams(vmem_limit_bytes=VMEM),
-        cost_estimate=pl.CostEstimate(
-            flops=4 * products, bytes_accessed=16 * steps * rows * width, transcendentals=steps * rows * units
-        ),
+        cost_estimate=pl.CostEstimate(flops=0, bytes_accessed=0, transcendentals=0),
     )(*operands)
 
 
@@ -1044,15 +1046,62 @@
     return jnp.concatenate([pick(pick(value, 1, near), 0, 1 - core), pick(got, 0, 1 - core)], axis=0)
 
 
-def own_pieces(value, got, last, core, near):
-    got = got.reshape((2,) + value.shape[2:])
-    last = last.reshape((2,) + value.shape[2:])
-    return [pick(pick(value, 1, near), 0, core), last[0], pick(got, 0, core), last[1]]
-
-
-def by_quarter(pieces, quarter, rows):
-    stacked = jnp.stack([piece[:rows] for piece in pieces])
-    return jnp.stack([pick(stacked, 0, quarter ^ k) for k in range(N)])
+def quarters(quarter, line, got, last, core, near):
+    size = line.shape[2]
+    mine = chosen(2 * core + near, [line[0, 0], line[0, 1], line[1, 0], line[1, 1]])
+    pieces = [mine, last[:size], jnp.where(core == 0, got[:size], got[size : 2 * size]), last[size : 2 * size]]
+    return [chosen(quarter ^ k, pieces) for k in range(N)]
+
+
+def finish_kernel(spot_ref, line_ref, got_ref, last_ref, reduce_ref, expand_out, dense_out, reduce_out):
+    core, near, half = spot_ref[0], spot_ref[1], spot_ref[2]
+    pieces = quarters(2 * near + core, wide(line_ref[...]), wide(got_ref[...]), wide(last_ref[...]), core, near)
+    rows = expand_out.shape[0]
+    for e in range(pieces[0].shape[1] // 128):
+        for slot in range(N):
+            piece = pieces[slot ^ (2 * (e % 2))]
+            to = (N * e + slot) * 128
+            expand_out[:, to : to + 128] = piece[:rows, e * 128 : (e + 1) * 128]
+    dense_out[...] = chosen(2 * core + half, [piece[rows:] for piece in pieces])
+    reduce_out[...] = wide(reduce_ref[...])
+
+
+def finish(spot, line, got, last, reduced):
+    rows, width = line.shape[2] // 2, line.shape[3]
+    return pl.pallas_call(
+        finish_kernel,
+        in_specs=[pl.BlockSpec(memory_space=pltpu.SMEM)] + [pl.BlockSpec(memory_space=pltpu.VMEM)] * 4,
+        out_specs=[pl.BlockSpec(memory_space=pltpu.VMEM)] * 3,
+        out_shape=[
+            jax.ShapeDtypeStruct((rows, N * width), jnp.float32),
+            jax.ShapeDtypeStruct((rows, width), jnp.float32),
+            jax.ShapeDtypeStruct(reduced.shape, jnp.float32),
+        ],
+        compiler_params=pltpu.CompilerParams(vmem_limit_bytes=VMEM),
+    )(spot, line, got, last, reduced)
+
+
+def joint_finish_kernel(spot_ref, line_ref, got_ref, last_ref, out_ref):
+    core, near = spot_ref[0], spot_ref[1]
+    pieces = quarters(2 * near + core, wide(line_ref[...]), wide(got_ref[...]), wide(last_ref[...]), core, near)
+    for n in range(pieces[0].shape[1] // (2 * HEAD)):
+        for slot in range(0, N, 2):
+            for other in range(2):
+                at = (2 * n + other) * HEAD
+                to = ((2 * n + other) * N + slot) * HEAD
+                pair = [piece[:, at : at + HEAD] for piece in pieces[slot : slot + 2]]
+                out_ref[:, to : to + 2 * HEAD] = jnp.concatenate(pair, axis=1)
+
+
+def joint_finish(spot, line, got, last):
+    rows, width = line.shape[2:]
+    return pl.pallas_call(
+        joint_finish_kernel,
+        in_specs=[pl.BlockSpec(memory_space=pltpu.SMEM)] + [pl.BlockSpec(memory_space=pltpu.VMEM)] * 3,
+        out_specs=pl.BlockSpec(memory_space=pltpu.VMEM),
+        out_shape=jax.ShapeDtypeStruct((rows, N * width), jnp.float32),
+        compiler_params=pltpu.CompilerParams(vmem_limit_bytes=VMEM),
+    )(spot, line, got, last)
 
 
 def split_local(
@@ -1109,17 +1158,17 @@
 
     spots = [z, z ^ (2 - flag), z ^ (1 + flag), z ^ 3]
     zero, one = jnp.int32(0), jnp.int32(1)
-    state = run_tokens(0, jnp.stack([spots[0], 1 - flag]), own_x, x_other, weights, tables, None)
+    state = run_tokens(0, jnp.stack([spots[0], 1 - flag]), [own_x, x_other], weights, tables, None)
     x_first, *state = tie(x_first, *state)
+    x_second = hop(x_first, NEAR_OFF)
     x_first_other = hop(x_first, CORE_SWAP)
-    x_second = hop(x_first, NEAR_OFF)
-    state = run_tokens(1, jnp.stack([spots[1], zero]), x_first, x_first, weights, tables, state)
-    x_first_other, x_second, own_g_late, *state = tie(x_first_other, x_second, own_g, *state)
+    state = run_tokens(1, jnp.stack([spots[1], zero]), [x_first], weights, tables, state)
+    x_second, own_g_late, *state = tie(x_second, own_g, *state)
+    x_second_other = hop(x_second, TO_MAIN)
     g_first = hop(own_g_late, HOME)
     g_other = hop(own_g_late, FROM_MAIN)
-    x_second_other = hop(x_second, TO_MAIN)
-    state = run_tokens(2, jnp.stack([spots[2], zero]), x_first_other, x_first_other, weights, tables, state)
-    state = run_tokens(3, jnp.stack([spots[3], 1 - flag]), x_second_other, x_second, weights, tables, state)
+    spot = jnp.stack([spots[2], spots[3], zero, 2 - flag])
+    state = run_tokens(2, spot, [x_first_other, x_second_other, x_second], weights, tables, state)
     qkv, unit, second, active, slope, feed = state
     order = z ^ (jnp.arange(N, dtype=jnp.int32) ^ (2 * flag))
     qkv = qkv.reshape(3, heads, HEAD, total)
@@ -1128,13 +1177,13 @@
     g_second = hop(g_first, NEAR_OFF)
     g_first_other = hop(g_first, CORE_SWAP)
     mixed, full, inverse_sum, shares = attend_forward(qkv, kx, qx, heads // 2, heads // 2, attended)
+    g_second, mixed = tie(g_second, mixed)
     mixed = mixed.reshape(-1, total)
+    g_second_other = hop(g_second, TO_MAIN)
     out_send, out_keep = deliver(order, mixed, wd, feed)
-    g_second, out_send, out_keep = tie(g_second, out_send, out_keep)
 
     spot = jnp.stack([*spots, 1 - flag, 2 * one, 3 * one, 5 - flag])
     spot, out_send, out_keep = tie(spot, out_send, out_keep)
-    g_second_other = hop(g_second, TO_MAIN)
     out_got = hop(out_send, CORE_SWAP)
     gs = (own_g, g_other, g_first, g_first_other, g_second_other, g_second)
     mg, back, ups, hg, sums, hsum = run_upstream(spot, gs, [wd, we, wr, second_row], unit, slope)
@@ -1163,7 +1212,6 @@
     send, keep = deliver(order, jb, wj, back, first_row)
 
     send, out_got_home, *shares_got = tie(send, out_got_home, *shares_got)
-    got = hop(send, CORE_SWAP)
     share = wide(kept_share) + sum(wide(piece) for piece in shares_got)
     kept = near ^ half
     part = width // 4
@@ -1172,12 +1220,13 @@
     dense_part = share[part + units // (4 * N) :]
     far_send = [pick(expand_part, 1, 1 - half).reshape(part // 2, -1), pick(reduce_part, 0, 1 - kept), dense_part]
     far_send = low(jnp.concatenate(far_send, axis=0))
+    far_send, send = tie(far_send, send)
+    got = hop(send, CORE_SWAP)
     far_got = hop(far_send, FAR_SWAP)
     near_part = near_sum(keep, got)
     out = own_sum(out_keep, out_got, out_got_home, main)
     inputs = wide(own_x)
     result = low(inputs + out + (dense_bias + reduce_bias))
-    near_part, result = tie(near_part, result)
     got_near = hop(near_part, NEAR_OFF)
 
     got_near, *joint_got = tie(got_near, *joint_got)
@@ -1188,11 +1237,15 @@
     joint_far_send = jnp.concatenate(
         [low(pick(joint_part, 1, 1 - half)).reshape(part // 2, joint_width), pack(vector, joint_width)], axis=0
     )
+    home = home_sum(keep, got, near_part, got_near, main)
+    home, joint_far_send, result = tie(home, joint_far_send, result)
+    got_home = hop(home, HOME)
+    joint_far = hop(joint_far_send, FAR_SWAP)
+    home, far_got = tie(home, far_got)
     far_got = wide(far_got)
     expand_part = low(pick(expand_part, 1, half).reshape(part // 2, -1) + far_got[: part // 2])
     reduce_part = low(pick(reduce_part, 0, kept) + far_got[part // 2 : part // 2 + 128])
     dense_part = low(dense_part + far_got[part // 2 + 128 :]).reshape(2, HEAD // 2, width)
-    home = home_sum(keep, got, near_part, got_near, main)
     line = jnp.concatenate(
         [
             expand_part.reshape(2, 2, part // 8, -1),
@@ -1201,23 +1254,8 @@
         axis=2,
     )
     line_send = first_pieces(line, near)
-    home, joint_far_send, line_send, reduce_part = tie(home, joint_far_send, line_send, reduce_part)
     line_got = hop(line_send, NEAR)
     reduce_got = hop(reduce_part, [((c, s), ((s % 2) ^ (s // 2), 2 * (s // 2) + c)) for c, s in PLACES])
-    got_home = hop(home, HOME)
-    joint_far = hop(joint_far_send, FAR_SWAP)
-    line_last = hop(second_pieces(line, line_got, core, near), CORE_SWAP)
-    line_mine = own_pieces(line, line_got, line_last, core, near)
-    expand_got = by_quarter(line_mine, quarter, part // 8)
-    dense_got = pick(jnp.stack([piece[part // 8 :] for piece in line_mine]), 0, 2 * (near ^ core) + (core ^ half))
-    expand_mine = expand_got.reshape(2, 2, -1, groups // 2, 2, 128)
-    expand_mine = jnp.stack([expand_mine[:, :, :, :, 0], expand_mine[::-1, :, :, :, 1]], axis=4)
-    expand_mine = wide(jnp.transpose(expand_mine, (2, 3, 4, 0, 1, 5)).reshape(-1, units))
-    reduce_mine = wide(reduce_got)
-    dense_mine = wide(dense_got)
-
-    joint_part = low(pick(joint_part, 1, half).reshape(part // 2, joint_width) + wide(joint_far[: part // 2]))
-    vector = vector + unpack(joint_far[part // 2 :], width)
     scaled = own_sum(keep, got, got_home, main)
     _, unit_rows, inverse_root = normalize(inputs, first_gain, first_shift)
     input_back = inverse_root * (
@@ -1226,20 +1264,22 @@
         - unit_rows * jnp.mean(scaled * unit_rows, axis=-1, keepdims=True)
     )
     tokens_gradient = low(wide(own_g) + input_back)
-    joint_part, vector, expand_mine, reduce_mine, dense_mine, tokens_gradient = tie(
-        joint_part, vector, expand_mine, reduce_mine, dense_mine, tokens_gradient
-    )
-    line = joint_part.reshape(2, 2, part // 8, joint_width)
-    line_got = hop(jnp.concatenate([first_pieces(line, near), pack(vector, joint_width)], axis=0), NEAR)
-    vector = vector + unpack(line_got[part // 4 :], width)
-    line_got = line_got[: part // 4]
-    line_last = hop(
-        jnp.concatenate([second_pieces(line, line_got, core, near), pack(vector, joint_width)], axis=0), CORE_SWAP
-    )
-    vector = vector + unpack(line_last[part // 4 :], width)
-    joint_mine = by_quarter(own_pieces(line, line_got, line_last[: part // 4], core, near), quarter, part // 8)
-    joint_mine = joint_mine.reshape(N, -1, 3, heads, HEAD)
-    joint_mine = wide(jnp.transpose(joint_mine, (1, 2, 3, 0, 4)).reshape(-1, 3 * width))
+    line_got, reduce_got, tokens_gradient = tie(line_got, reduce_got, tokens_gradient)
+    line_send = second_pieces(line, line_got, core, near)
+    line_last = hop(line_send, CORE_SWAP)
+    joint_far, line_send = tie(joint_far, line_send)
+    joint_part = low(pick(joint_part, 1, half).reshape(part // 2, joint_width) + wide(joint_far[: part // 2]))
+    vector = vector + unpack(joint_far[part // 2 :], width)
+    joint_line = joint_part.reshape(2, 2, part // 8, joint_width)
+    joint_got = hop(jnp.concatenate([first_pieces(joint_line, near), pack(vector, joint_width)], axis=0), NEAR)
+    spot = jnp.stack([core, near, half])
+    expand_mine, dense_mine, reduce_mine = finish(spot, line, line_got, line_last, reduce_got)
+    joint_got, expand_mine = tie(joint_got, expand_mine)
+    vector = vector + unpack(joint_got[part // 4 :], width)
+    joint_send = second_pieces(joint_line, joint_got[: part // 4], core, near)
+    joint_last = hop(jnp.concatenate([joint_send, pack(vector, joint_width)], axis=0), CORE_SWAP)
+    vector = vector + unpack(joint_last[part // 4 :], width)
+    joint_mine = joint_finish(spot, joint_line, joint_got, joint_last)
 
     device = (2 * col + core) * N + z
     share = width // (8 * N)

time: 339 us -> 315 us (0.929)
  waiting for transfers between devices: 69.1 us -> 46.6 us
  starting transfers between devices: 46.2 us -> 58.8 us
  local copies, waits for them, and re-layouts: 21 us -> 12.5 us
  other arithmetic: 28.6 us -> 23.9 us
    ppermute x24, waiting for transfers between devices: 67.9 us -> 29.9 us  [hop(): lax.ppermute(value, ('core', 'blk'), [(a[0] * N + a[1], b[0] * N + b[1])...]
    ppermute x6, waiting for transfers between devices: 1.19 us -> 16.7 us  [plane(): lax.ppermute(value, 'col', [(i, i ^ k + 1) for i in range(4)])]
    ppermute x24, starting transfers between devices: 39.1 us -> 51.8 us  [hop(): lax.ppermute(value, ('core', 'blk'), [(a[0] * N + a[1], b[0] * N + b[1])...]
    pallas_call x0 -> x2, Pallas kernels: none -> 4.53 us  [the longest x1 2.5 us: finish(): pl.pallas_call(finish_kernel, in_specs=[pl.BlockSpec(memory_space=pltpu.S...]
    convert_element_type x4 -> x0, local copies, waits for them, and re-layouts: 4.44 us -> none  [wide(): return value.astype(jnp.float32)]
    pallas_call x4 -> x3, Pallas kernels: 41.8 us -> 37.8 us  [run_tokens(): pl.pallas_call(partial(token_kernel, len(data), sub, chunk), grid_spec=pl...]
  transfers between devices with their start and end apart: 30 -> 30, of which waited for: 5 -> 11; matrix products, arithmetic and copies ran while one was open for 9% -> 7% of each run, Pallas kernels for 50% -> 53%
where the time goes in v2:
time: 315 us; the launch traced here: 309 us
  Pallas kernels  165 us (52%)
  starting transfers between devices  58.8 us (19%)
  waiting for transfers between devices  46.6 us (15%)
  other arithmetic  23.9 us (8%)
  local copies, waits for them, and re-layouts  12.5 us (4%)
    ppermute x24, starting transfers between devices, hop(): lax.ppermute(value, ('core', 'blk'), [(a[0] * N + a[1], b[0] * N + b[1])...  51.8 us
    pallas_call x3, Pallas kernels, run_tokens(): pl.pallas_call(partial(token_kernel, len(data), sub, chunk), grid_spec=pl...  37.8 us
    ppermute x24, waiting for transfers between devices, hop(): lax.ppermute(value, ('core', 'blk'), [(a[0] * N + a[1], b[0] * N + b[1])...  29.9 us
    pallas_call x1, Pallas kernels, attend_backward(): pl.pallas_call(backward_kernel, grid=(heads,), in_specs=[kinds, head_rows...  26.4 us
    pallas_call x2, Pallas kernels, attend_forward(): pl.pallas_call(partial(forward_kernel, len(aliases)), grid=(count,), in_s...  23.3 us
    pallas_call x1, Pallas kernels, run_upstream(): pl.pallas_call(partial(upstream_kernel, chunk), grid_spec=pltpu.PrefetchS...  18.6 us
    pallas_call x1, Pallas kernels, weight_gradients(): pl.pallas_call(weight_kernel, grid_spec=pltpu.PrefetchScalarGridSpec(num_...  16.8 us
    ppermute x6, waiting for transfers between devices, plane(): lax.ppermute(value, 'col', [(i, i ^ k + 1) for i in range(4)])  16.7 us
  transfers between devices with their start and end apart: 30, of which 11 were waited for; matrix products, arithmetic and copies ran while one was open for 7% of the time, Pallas kernels for 53%

profile of v2, /device:TPU:0, one launch (start us, length us, event | category | flops | bytes accessed | tf_op | source)
XLA Modules:
  0.0 309.1 jit_solution(11096144199555950730)
XLA Ops:
  0.6 2.4 collective-permute-start.1
  3.1 2.5 collective-permute-start
  10.0 10.4 %shard_map.262 = (bf16[768,1024]{1,0:T(8,128)(2,1)}, bf16[256,1024]{1,0:T(8,128)(2,1)}, bf16[1024,1024]{1,0:T(8,128)(2,1)}, bf16[1024,1024]{1,0:T(8,128)(2,1)}) custom-call(s32[1]{0:T(128)} %bitcast.6.spot_ref, bf16[1024,3072]{1,0:T(8,128)(2,1)} %wj_ref.1, bf16[1024,1024]{1,0:T(8,128)(2,1)} %wd_ref.1, bf16[1024,4096]{1,0:T(8,128)(2,1)} %we_ref.1, ...), custom_call_target="tpu_custom_call" | custom-call | bytes 14680064 | tf_op jit(solution)/shard_map/pallas_call | solution.py:392
  22.8 10.6 %shard_map.263 = (bf16[768,2048]{1,0:T(8,128)(2,1)}, bf16[2048,1024]{1,0:T(8,128)(2,1)}, bf16[2048,1024]{1,0:T(8,128)(2,1)}, bf16[2048,1024]{1,0:T(8,128)(2,1)},...) custom-call(s32[2]{0:T(128)} %pad_add_fusion.1.spot_ref, bf16[512,1024]{1,0:T(8,128)(2,1)} %bitcast.95, ...), custom_call_target="tpu_custom_call" | custom-call | tf_op jit(solution)/shard_map/pallas_call | solution.py:672
  35.1 2.5 collective-permute-start.3
  37.5 10.2 %shard_map.264 = (bf16[768,2048]{1,0:T(8,128)(2,1)}, bf16[2048,1024]{1,0:T(8,128)(2,1)}, bf16[2048,1024]{1,0:T(8,128)(2,1)}, bf16[2048,1024]{1,0:T(8,128)(2,1)},...) custom-call(s32[2]{0:T(128)} %pad_add_fusion.2.spot_ref, ...), custom_call_target="tpu_custom_call", output_to_operand_aliasing={{0}: (13, {}), {1}: (14, {}), {2}: (15, {}), {3}: (16, {}),... | custom-call | tf_op jit(solution)/shard_map/pallas_call | solution.py:672
  47.7 1.8 collective-permute-start.5
  52.5 17.0 %shard_map.265 = (bf16[768,2048]{1,0:T(8,128)(2,1)}, bf16[2048,1024]{1,0:T(8,128)(2,1)}, bf16[2048,1024]{1,0:T(8,128)(2,1)}, bf16[2048,1024]{1,0:T(8,128)(2,1)},...) custom-call(s32[4]{0:T(128)} %pad_add_fusion.spot_ref, ...), custom_call_target="tpu_custom_call", output_to_operand_aliasing={{0}: (15, {}), {1}: (16, {}), {2}: (17, {}), {3}: (18, {}),... | custom-call | tf_op jit(solution)/shard_map/pallas_call | solution.py:672
  69.5 11.7 %shard_map.266 = (bf16[4,64,2048]{2,1,0:T(8,128)(2,1)}, f32[4,64,2048]{2,1,0:T(8,128)}, f32[4,1,2048]{2,1,0:T(1,128)}, bf16[4,10,512,512]{3,2,1,0:T(8,128)(2,1)}) custom-call(bf16[3,4,64,2048]{3,2,1,0:T(8,128)(2,1)} %bitcast.90, bf16[64,2048]{1,0:T(8,128)(2,1)} %get-tuple-element.278.kx_ref, bf16[64,2048]{1,0:T(8,128)(2,1)} %get-tuple-element.277.qx_ref), custom_call_target="tpu_custom_call" | custom-call | flops 5368709120 | bytes 10485760 | tf_op jit(solution)/shard_map/pallas_call | solution.py:490
  81.2 1.6 collective-permute-start.7
  82.8 8.2 %collective-permute-start.9 = (bf16[512,1024]{1,0:T(8,128)(2,1)S(1)}, bf16[512,1024]{1,0:T(8,128)(2,1)}, u32[]{:S(2)}, u32[]{:S(2)}) collective-permute-start(bf16[512,1024]{1,0:T(8,128)(2,1)S(1)} %bitcast.100), channel_id=1, source_target_pairs={{0,4},{1,5},{6,2},{7,3},{8,12},{9,13},{14,10},{15,11},{16,20},{17,... | collective-permute-start | bytes 3145736 | tf_op jit(solution)/shard_map/ppermute | solution.py:992
  91.2 11.7 %shard_map.267 = (bf16[4,64,2048]{2,1,0:T(8,128)(2,1)}, f32[4,64,2048]{2,1,0:T(8,128)}, f32[4,1,2048]{2,1,0:T(1,128)}, bf16[4,10,512,512]{3,2,1,0:T(8,128)(2,1)}) custom-call(bf16[3,4,64,2048]{3,2,1,0:T(8,128)(2,1)} %bitcast.91, bf16[64,2048]{1,0:T(8,128)(2,1)} %get-tuple-element.278.kx_ref, ...), custom_call_target="tpu_custom_call", output_to_operand_aliasing={{0}: (3, {}), {1}: (4, {}), {2}: (5, {}), {3}: (6, {})} | custom-call | flops 5368709120 | bytes 10485760 | tf_op jit(solution)/shard_map/pallas_call | solution.py:490
  102.8 1.3 collective-permute-start.11
  105.3 7.0 %shard_map.268 = (bf16[1024,1024]{1,0:T(8,128)(2,1)}, bf16[1024,1024]{1,0:T(8,128)(2,1)}) custom-call(s32[4]{0:T(128)} %xor_xor_fusion.order_ref, bf16[256,2048]{1,0:T(8,128)(2,1)} %bitcast.104, bf16[256,1024]{1,0:T(8,128)(2,1)} %get-tuple-element.166.weight_ref.refs_6_, bf16[2048,1024]{1,0:T(8,128)(2,1)} %get-tuple-element.167.add_ref), custom_call_target="tpu_custom_call" | custom-call | tf_op jit(solution)/shard_map/pallas_call | solution.py:868
  112.3 2.1 collective-permute-start.8
  116.3 18.6 %shard_map.269 = (bf16[256,2048]{1,0:T(8,128)(2,1)}, bf16[2048,1024]{1,0:T(8,128)(2,1)}, bf16[2048,1024]{1,0:T(8,128)(2,1)}, bf16[2048,1024]{1,0:T(8,128)(2,1)},...) custom-call(s32[8]{0:T(128)} %stack.81.spot_ref, bf16[512,1024]{1,0:T(8,128)(2,1)} %bitcast.98, ...), custom_call_target="tpu_custom_call" | custom-call | flops 14495514624 | bytes 25165824 | tf_op jit(solution)/shard_map/pallas_call | solution.py:752
  136.3 16.8 %shard_map.270 = (bf16[576,1024]{1,0:T(8,128)(2,1)}, bf16[576,1024]{1,0:T(8,128)(2,1)}, bf16[576,1024]{1,0:T(8,128)(2,1)}, bf16[576,1024]{1,0:T(8,128)(2,1)}) custom-call(s32[5]{0:T(128)} %stack.83.spot_ref, bf16[2048,1024]{1,0:T(8,128)(2,1)} %get-tuple-element.179.second_ref, bf16[2048,1024]{1,0:T(8,128)(2,1)} %get-tuple-element.180.hg_ref, ...), custom_call_target="tpu_custom_call" | custom-call | flops 14495514624 | bytes 16777216 | tf_op jit(solution)/shard_map/pallas_call | solution.py:808
  153.1 1.9 fusion.12
  154.9 1.5 collective-permute-start.14
  156.4 1.5 collective-permute-start.15
  158.4 1.5 collective-permute-start.13
  160.0 26.4 %shard_map.271 = bf16[3,4,64,2048]{3,2,1,0:T(8,128)(2,1)} custom-call(bf16[3,4,64,2048]{3,2,1,0:T(8,128)(2,1)} %bitcast.92, bf16[4,64,2048]{2,1,0:T(8,128)(2,1)} %bitcast.145, f32[4,64,2048]{2,1,0:T(8,128)} %get-tuple-element.187.full_ref, f32[4,1,2048]{2,1,0:T(1,128)} %get-tuple-element.188.inverse_ref, ...), custom_call_target="tpu_custom_call" | custom-call | flops 21474836480 | bytes 20971520 | tf_op jit(solution)/shard_map/pallas_call | solution.py:571
  186.4 10.7 %shard_map.272 = (bf16[256,768]{1,0:T(8,128)(2,1)}, bf16[320,768]{1,0:T(8,128)(2,1)}, bf16[320,768]{1,0:T(8,128)(2,1)}, bf16[320,768]{1,0:T(8,128)(2,1)}, f32[16,1024]{1,0:T(8,128)}) custom-call(s32[2]{0:T(128)} %pad_add_fusion.3.spot_ref, bf16[768,2048]{1,0:T(8,128)(2,1)} %bitcast.96, bf16[2048,1024]{1,0:T(8,128)(2,1)} %get-tuple-element.174.refs_10_.unit_ref, ...), custom_call_target="tpu_custom_call" | custom-call | tf_op jit(solution)/shard_map/pallas_call | solution.py:946
  197.1 9.7 %shard_map.273 = (bf16[1024,1024]{1,0:T(8,128)(2,1)}, bf16[1024,1024]{1,0:T(8,128)(2,1)}) custom-call(s32[4]{0:T(128)} %xor_xor_fusion.order_ref, bf16[768,2048]{1,0:T(8,128)(2,1)} %bitcast.97, bf16[768,1024]{1,0:T(8,128)(2,1)} %get-tuple-element.124.refs_2_.refs_1_.refs_3_.wj_ref.weight_ref, bf16[2048,1024]{1,0:T(8,128)(2,1)} %get-tuple-element.196.add_ref, ...), custom_call_target="tpu_custom_call" | custom-call | tf_op jit(solution)/shard_map/pallas_call | solution.py:868
  206.8 2.0 collective-permute-done.16
  212.3 1.8 collective-permute-start.17
  214.1 3.8 %collective-permute-done.17 = bf16[1024,1024]{1,0:T(8,128)(2,1)S(1)} collective-permute-done((bf16[1024,1024]{1,0:T(8,128)(2,1)S(1)}, bf16[1024,1024]{1,0:T(8,128)(2,1)S(1)}, u32[]{:S(2)}, u32[]{:S(2)}) %collective-permute-start.17) | collective-permute-done | bytes 2097184 | tf_op jit(solution)/shard_map/ppermute | solution.py:992
  217.9 1.6 add_convert_fusion.1
  219.5 1.6 collective-permute-start.18
  224.1 1.4 collective-permute-start.21
  225.5 1.9 collective-permute-start.22
  228.5 3.4 %fusion.9 = (f32[512]{0:T(512)S(1)}, bf16[512,1024]{1,0:T(8,128)(2,1)}) fusion(f32[512]{0:T(512)S(1)} %broadcast_multiply_fusion.2, bf16[1,512,1024]{2,1,0:T(8,128)(2,1)S(1)} %copy-done, f32[1024]{0:T(1024)S(1)} %add.317, bf16[512,1024]{1,0:T(8,128)(2,1)} %copy-done.17, bf16[1024,1024]{1,0:T(8,128)(2,1)} %copy-done.7, bf16[1024,1024]{1,0:T(8,128)(2,1)S(1)} %copy-done.6, ...), kind=kLoop, calls=%fused_computation.13 | loop fusion | flops 6815232 | bytes 5251073 | tf_op jit(solution)/shard_map/reduce_sum | solution.py:57
  231.9 3.2 %collective-permute-done.19 = bf16[320,768]{1,0:T(8,128)(2,1)S(1)} collective-permute-done((bf16[320,768]{1,0:T(8,128)(2,1)}, bf16[320,768]{1,0:T(8,128)(2,1)S(1)}, u32[]{:S(2)}, u32[]{:S(2)}) %collective-permute-start.19) | collective-permute-done | bytes 491552 | tf_op jit(solution)/shard_map/ppermute | solution.py:1034
  235.1 1.9 collective-permute-done.20
  237.1 9.5 %collective-permute-done.21 = bf16[320,768]{1,0:T(8,128)(2,1)S(1)} collective-permute-done((bf16[320,768]{1,0:T(8,128)(2,1)}, bf16[320,768]{1,0:T(8,128)(2,1)S(1)}, u32[]{:S(2)}, u32[]{:S(2)}) %collective-permute-start.21) | collective-permute-done | bytes 491552 | tf_op jit(solution)/shard_map/ppermute | solution.py:1034
  249.0 2.4 fusion.13
  251.4 2.8 collective-permute-start.25
  254.2 4.5 %collective-permute-done.22 = bf16[320,1024]{1,0:T(8,128)(2,1)S(1)} collective-permute-done((bf16[320,1024]{1,0:T(8,128)(2,1)}, bf16[320,1024]{1,0:T(8,128)(2,1)S(1)}, u32[]{:S(2)}, u32[]{:S(2)}) %collective-permute-start.22) | collective-permute-done | bytes 655392 | tf_op jit(solution)/shard_map/ppermute | solution.py:992
  259.2 3.8 %collective-permute-start.23 = (bf16[128,1024]{1,0:T(8,128)(2,1)S(1)}, bf16[128,1024]{1,0:T(8,128)(2,1)S(1)}, u32[]{:S(2)}, u32[]{:S(2)}) collective-permute-start(bf16[128,1024]{1,0:T(8,128)(2,1)S(1)} %bitcast.122), channel_id=1, source_target_pairs={{0,1},{1,0},{2,3},{3,2},{4,5},{5,4},{6,7},{7,6},{8,9},{9,8},{10,11... | collective-permute-start | bytes 786440 | tf_op jit(solution)/shard_map/ppermute | solution.py:992
  263.7 5.1 %collective-permute-start.26 = (bf16[192,768]{1,0:T(8,128)(2,1)S(1)}, bf16[192,768]{1,0:T(8,128)(2,1)S(1)}, u32[]{:S(2)}, u32[]{:S(2)}) collective-permute-start(bf16[192,768]{1,0:T(8,128)(2,1)S(1)} %constant_dynamic-update-slice_fusion), channel_id=1, source_target_pairs={{0,2},{1,3},{2,0},{3,1},{4,6},{5,7},{6,4},{7,5},{8,10},{9,11},{10,... | collective-permute-start | bytes 884744 | tf_op jit(solution)/shard_map/ppermute | solution.py:992
  268.8 11.5 %collective-permute-done.25 = bf16[512,1024]{1,0:T(8,128)(2,1)S(1)} collective-permute-done((bf16[512,1024]{1,0:T(8,128)(2,1)S(1)}, bf16[512,1024]{1,0:T(8,128)(2,1)S(1)}, u32[]{:S(2)}, u32[]{:S(2)}) %collective-permute-start.25) | collective-permute-done | bytes 1048608 | tf_op jit(solution)/shard_map/ppermute | solution.py:992
  281.3 2.1 fusion.8
  283.4 5.1 %collective-permute-done.23.got_ref = bf16[128,1024]{1,0:T(8,128)(2,1)S(1)} collective-permute-done((bf16[128,1024]{1,0:T(8,128)(2,1)S(1)}, bf16[128,1024]{1,0:T(8,128)(2,1)S(1)}, u32[]{:S(2)}, u32[]{:S(2)}) %collective-permute-start.23) | collective-permute-done | bytes 262176 | tf_op jit(solution)/shard_map/ppermute | solution.py:992
  288.6 6.8 %collective-permute-start.28 = (bf16[128,1024]{1,0:T(8,128)(2,1)S(1)}, bf16[128,1024]{1,0:T(8,128)(2,1)S(1)}, u32[]{:S(2)}, u32[]{:S(2)}) collective-permute-start(bf16[128,1024]{1,0:T(8,128)(2,1)S(1)} %pad_maximum_fusion.2), channel_id=1, source_target_pairs={{0,4},{1,5},{2,6},{3,7},{4,0},{5,1},{6,2},{7,3},{8,12},{9,13},{10,... | collective-permute-start | bytes 786440 | tf_op jit(solution)/shard_map/ppermute | solution.py:992
  297.3 2.5 shard_map.274
  299.8 2.8 collective-permute-done.27.got_ref
  302.9 1.3 collective-permute-done.29.last_ref
  306.1 2.0 shard_map.275
  (195 shorter events, 32.3 us)
Async XLA Ops:
  0.6 21.2 %collective-permute-start.1 = (bf16[512,1024]{1,0:T(8,128)(2,1)}, bf16[512,1024]{1,0:T(8,128)(2,1)S(1)}, u32[]{:S(2)}, u32[]{:S(2)}) collective-permute-start(bf16[512,1024]{1,0:T(8,128)(2,1)} %bitcast.93), channel_id=1, source_target_pairs={{0,4},{1,5},{6,2},{7,3},{8,12},{9,13},{14,10},{15,11},{16,20},{17,... | collective-permute-start | bytes 3145736 | tf_op jit(solution)/shard_map/ppermute | solution.py:992
  3.1 30.3 %collective-permute-start = (bf16[512,1024]{1,0:T(8,128)(2,1)}, bf16[512,1024]{1,0:T(8,128)(2,1)S(1)}, u32[]{:S(2)}, u32[]{:S(2)}) collective-permute-start(bf16[512,1024]{1,0:T(8,128)(2,1)} %bitcast.94), channel_id=1, source_target_pairs={{0,1},{1,0},{6,7},{7,6},{2,4},{3,5},{4,2},{5,3},{8,9},{9,8},{14,15... | collective-permute-start | bytes 3145736 | tf_op jit(solution)/shard_map/ppermute | solution.py:992
  5.5 14.9 %collective-permute-start.2 = (s32[1,4]{1,0:T(1,128)}, s32[1,4]{1,0:T(1,128)S(1)}, u32[]{:S(2)}, u32[]{:S(2)}) collective-permute-start(s32[1,4]{1,0:T(1,128)} %param.16), channel_id=1, source_target_pairs={{0,4},{1,5},{2,6},{3,7},{4,0},{5,1},{6,2},{7,3},{8,12},{9,13},{10,... | collective-permute-start | bytes 56 | tf_op jit(solution)/shard_map/ppermute | solution.py:992
  10.0 10.4 %copy-start.28 = (s32[1,4]{1,0:T(1,128)S(1)}, s32[1,4]{1,0:T(1,128)}, u32[]{:S(2)}) copy-start(s32[1,4]{1,0:T(1,128)} %param.16) | copy-start | bytes 52
  33.4 4.1 %copy-start.15 = (bf16[512,1024]{1,0:T(8,128)(2,1)}, bf16[512,1024]{1,0:T(8,128)(2,1)S(1)}, u32[]{:S(2)}) copy-start(bf16[512,1024]{1,0:T(8,128)(2,1)S(1)} %collective-permute-done.refs_0_) | copy-start | bytes 3145732
  33.4 14.3 %collective-permute-start.4 = (bf16[512,1024]{1,0:T(8,128)(2,1)S(1)}, bf16[512,1024]{1,0:T(8,128)(2,1)S(1)}, u32[]{:S(2)}, u32[]{:S(2)}) collective-permute-start(bf16[512,1024]{1,0:T(8,128)(2,1)S(1)} %collective-permute-done.refs_0_), channel_id=1, source_target_pairs={{2,3},{3,2},{4,5},{5,4},{10,11},{11,10},{12,13},{13,12},{18,19},{1... | collective-permute-start | bytes 3145736 | tf_op jit(solution)/shard_map/ppermute | solution.py:992
  35.1 14.5 %copy-start.8 = (bf16[1,512,1024]{2,1,0:T(8,128)(2,1)S(1)}, bf16[1,512,1024]{2,1,0:T(8,128)(2,1)}, u32[]{:S(2)}) copy-start(bf16[1,512,1024]{2,1,0:T(8,128)(2,1)} %param.29) | copy-start | bytes 3145732
  35.1 16.7 %collective-permute-start.3 = (bf16[512,1024]{1,0:T(8,128)(2,1)S(1)}, bf16[512,1024]{1,0:T(8,128)(2,1)}, u32[]{:S(2)}, u32[]{:S(2)}) collective-permute-start(bf16[512,1024]{1,0:T(8,128)(2,1)S(1)} %collective-permute-done.refs_0_), channel_id=1, source_target_pairs={{0,4},{1,5},{2,6},{3,7},{4,0},{5,1},{6,2},{7,3},{8,12},{9,13},{10,... | collective-permute-start | bytes 3145736 | tf_op jit(solution)/shard_map/ppermute | solution.py:992
  47.7 4.8 %copy-start.16 = (bf16[512,1024]{1,0:T(8,128)(2,1)}, bf16[512,1024]{1,0:T(8,128)(2,1)S(1)}, u32[]{:S(2)}) copy-start(bf16[512,1024]{1,0:T(8,128)(2,1)S(1)} %collective-permute-done.4.refs_2_) | copy-start | bytes 3145732
  47.7 4.8 %collective-permute-start.5 = (bf16[512,1024]{1,0:T(8,128)(2,1)S(1)}, bf16[512,1024]{1,0:T(8,128)(2,1)}, u32[]{:S(2)}, u32[]{:S(2)}) collective-permute-start(bf16[512,1024]{1,0:T(8,128)(2,1)S(1)} %collective-permute-done.4.refs_2_), channel_id=1, source_target_pairs={{2,6},{3,7},{4,0},{5,1},{10,14},{11,15},{12,8},{13,9},{18,22},{19,... | collective-permute-start | bytes 3145736 | tf_op jit(solution)/shard_map/ppermute | solution.py:992
  49.6 31.6 %collective-permute-start.6 = (bf16[512,1024]{1,0:T(8,128)(2,1)S(1)}, bf16[512,1024]{1,0:T(8,128)(2,1)}, u32[]{:S(2)}, u32[]{:S(2)}) collective-permute-start(bf16[512,1024]{1,0:T(8,128)(2,1)S(1)} %bitcast.99), channel_id=1, source_target_pairs={{0,1},{1,0},{6,7},{7,6},{2,4},{3,5},{4,2},{5,3},{8,9},{9,8},{14,15... | collective-permute-start | bytes 3145736 | tf_op jit(solution)/shard_map/ppermute | solution.py:992
  81.2 21.6 %collective-permute-start.7 = (bf16[512,1024]{1,0:T(8,128)(2,1)}, bf16[512,1024]{1,0:T(8,128)(2,1)}, u32[]{:S(2)}, u32[]{:S(2)}) collective-permute-start(bf16[512,1024]{1,0:T(8,128)(2,1)} %collective-permute-done.6.refs_2_), channel_id=1, source_target_pairs={{2,3},{3,2},{4,5},{5,4},{10,11},{11,10},{12,13},{13,12},{18,19},{1... | collective-permute-start | bytes 3145736 | tf_op jit(solution)/shard_map/ppermute | solution.py:992
  82.8 33.5 %collective-permute-start.9 = (bf16[512,1024]{1,0:T(8,128)(2,1)S(1)}, bf16[512,1024]{1,0:T(8,128)(2,1)}, u32[]{:S(2)}, u32[]{:S(2)}) collective-permute-start(bf16[512,1024]{1,0:T(8,128)(2,1)S(1)} %bitcast.100), channel_id=1, source_target_pairs={{0,4},{1,5},{6,2},{7,3},{8,12},{9,13},{14,10},{15,11},{16,20},{17,... | collective-permute-start | bytes 3145736 | tf_op jit(solution)/shard_map/ppermute | solution.py:992
  91.1 25.2 %collective-permute-start.10 = (bf16[512,1024]{1,0:T(8,128)(2,1)}, bf16[512,1024]{1,0:T(8,128)(2,1)}, u32[]{:S(2)}, u32[]{:S(2)}) collective-permute-start(bf16[512,1024]{1,0:T(8,128)(2,1)} %collective-permute-done.6.refs_2_), channel_id=1, source_target_pairs={{0,4},{1,5},{2,6},{3,7},{4,0},{5,1},{6,2},{7,3},{8,12},{9,13},{10,... | collective-permute-start | bytes 3145736 | tf_op jit(solution)/shard_map/ppermute | solution.py:992
  102.8 13.5 %collective-permute-start.11 = (bf16[512,1024]{1,0:T(8,128)(2,1)}, bf16[512,1024]{1,0:T(8,128)(2,1)}, u32[]{:S(2)}, u32[]{:S(2)}) collective-permute-start(bf16[512,1024]{1,0:T(8,128)(2,1)} %collective-permute-done.7.refs_5_), channel_id=1, source_target_pairs={{2,6},{3,7},{4,0},{5,1},{10,14},{11,15},{12,8},{13,9},{18,22},{19,... | collective-permute-start | bytes 3145736 | tf_op jit(solution)/shard_map/ppermute | solution.py:992
  112.3 22.6 %collective-permute-start.8 = (bf16[1024,1024]{1,0:T(8,128)(2,1)}, bf16[1024,1024]{1,0:T(8,128)(2,1)S(1)}, u32[]{:S(2)}, u32[]{:S(2)}) collective-permute-start(bf16[1024,1024]{1,0:T(8,128)(2,1)} %get-tuple-element.171), channel_id=1, source_target_pairs={{0,4},{1,5},{2,6},{3,7},{4,0},{5,1},{6,2},{7,3},{8,12},{9,13},{10,... | collective-permute-start | bytes 6291464 | tf_op jit(solution)/shard_map/ppermute | solution.py:992
  116.3 18.6 %copy-start.5 = (bf16[1024,1024]{1,0:T(8,128)(2,1)S(1)}, bf16[1024,1024]{1,0:T(8,128)(2,1)}, u32[]{:S(2)}) copy-start(bf16[1024,1024]{1,0:T(8,128)(2,1)} %get-tuple-element.170) | copy-start | bytes 6291460
  134.9 18.1 %copy-start.7 = (bf16[1024,1024]{1,0:T(8,128)(2,1)}, bf16[1024,1024]{1,0:T(8,128)(2,1)S(1)}, u32[]{:S(2)}) copy-start(bf16[1024,1024]{1,0:T(8,128)(2,1)S(1)} %collective-permute-done.8) | copy-start | bytes 6291460
  135.3 17.7 %collective-permute-start.12 = (bf16[512,1024]{1,0:T(8,128)(2,1)S(1)}, bf16[512,1024]{1,0:T(8,128)(2,1)S(1)}, u32[]{:S(2)}, u32[]{:S(2)}) collective-permute-start(bf16[512,1024]{1,0:T(8,128)(2,1)S(1)} %add_convert_fusion.3), channel_id=1, source_target_pairs={{2,3},{3,2},{4,5},{5,4},{10,11},{11,10},{12,13},{13,12},{18,19},{1... | collective-permute-start | bytes 3145736 | tf_op jit(solution)/shard_map/ppermute | solution.py:992
  154.9 51.8 %collective-permute-start.14 = (bf16[576,1024]{1,0:T(8,128)(2,1)}, bf16[576,1024]{1,0:T(8,128)(2,1)S(1)}, u32[]{:S(2)}, u32[]{:S(2)}) collective-permute-start(bf16[576,1024]{1,0:T(8,128)(2,1)} %get-tuple-element.201), channel_id=1, source_target_pairs={{0,8},{8,0},{16,24},{24,16},{1,9},{9,1},{17,25},{25,17},{2,10},{10... | collective-permute-start | bytes 3538952 | tf_op jit(solution)/shard_map/ppermute | solution.py:1034
  156.4 50.4 %collective-permute-start.15 = (bf16[576,1024]{1,0:T(8,128)(2,1)}, bf16[576,1024]{1,0:T(8,128)(2,1)S(1)}, u32[]{:S(2)}, u32[]{:S(2)}) collective-permute-start(bf16[576,1024]{1,0:T(8,128)(2,1)} %get-tuple-element.202), channel_id=1, source_target_pairs={{0,16},{8,24},{16,0},{24,8},{1,17},{9,25},{17,1},{25,9},{2,18},{10... | collective-permute-start | bytes 3538952 | tf_op jit(solution)/shard_map/ppermute | solution.py:1034
  157.9 50.8 %collective-permute-start.16 = (bf16[576,1024]{1,0:T(8,128)(2,1)}, bf16[576,1024]{1,0:T(8,128)(2,1)S(1)}, u32[]{:S(2)}, u32[]{:S(2)}) collective-permute-start(bf16[576,1024]{1,0:T(8,128)(2,1)} %get-tuple-element.203), channel_id=1, source_target_pairs={{0,24},{8,16},{16,8},{24,0},{1,25},{9,17},{17,9},{25,1},{2,26},{10... | collective-permute-start | bytes 3538952 | tf_op jit(solution)/shard_map/ppermute | solution.py:1034
  158.4 48.3 %collective-permute-start.13 = (bf16[512,1024]{1,0:T(8,128)(2,1)}, bf16[512,1024]{1,0:T(8,128)(2,1)S(1)}, u32[]{:S(2)}, u32[]{:S(2)}) collective-permute-start(bf16[512,1024]{1,0:T(8,128)(2,1)} %fusion.12), channel_id=1, source_target_pairs={{0,1},{1,0},{6,7},{7,6},{2,4},{3,5},{4,2},{5,3},{8,9},{9,8},{14,15... | collective-permute-start | bytes 3145736 | tf_op jit(solution)/shard_map/ppermute | solution.py:992
  197.1 11.7 %copy-start.14 = (bf16[576,1024]{1,0:T(8,128)(2,1)S(1)}, bf16[576,1024]{1,0:T(8,128)(2,1)}, u32[]{:S(2)}) copy-start(bf16[576,1024]{1,0:T(8,128)(2,1)} %get-tuple-element.198) | copy-start | bytes 3538948
  210.0 7.8 %copy-start.1 = (bf16[1024,1024]{1,0:T(8,128)(2,1)S(1)}, bf16[1024,1024]{1,0:T(8,128)(2,1)}, u32[]{:S(2)}) copy-start(bf16[1024,1024]{1,0:T(8,128)(2,1)} %get-tuple-element.197) | copy-start | bytes 6291460
  211.3 9.8 %copy-start.26 = (f32[1024]{0:T(1024)S(1)}, f32[1024]{0:T(1024)}, u32[]{:S(2)}) copy-start(f32[1024]{0:T(1024)} %param.24) | copy-start | bytes 12292
  211.3 9.8 %copy-start.27 = (f32[1024]{0:T(1024)S(1)}, f32[1024]{0:T(1024)}, u32[]{:S(2)}) copy-start(f32[1024]{0:T(1024)} %param.28) | copy-start | bytes 12292
  211.3 10.4 %copy-start = (bf16[1,512,1024]{2,1,0:T(8,128)(2,1)S(1)}, bf16[1,512,1024]{2,1,0:T(8,128)(2,1)}, u32[]{:S(2)}) copy-start(bf16[1,512,1024]{2,1,0:T(8,128)(2,1)} %param.15) | copy-start | bytes 3145732
  212.3 5.6 %collective-permute-start.17 = (bf16[1024,1024]{1,0:T(8,128)(2,1)S(1)}, bf16[1024,1024]{1,0:T(8,128)(2,1)S(1)}, u32[]{:S(2)}, u32[]{:S(2)}) collective-permute-start(bf16[1024,1024]{1,0:T(8,128)(2,1)S(1)} %copy-done.30), channel_id=1, source_target_pairs={{0,4},{1,5},{2,6},{3,7},{4,0},{5,1},{6,2},{7,3},{8,12},{9,13},{10,... | collective-permute-start | bytes 6291464 | tf_op jit(solution)/shard_map/ppermute | solution.py:992
  219.5 27.1 %collective-permute-start.18 = (bf16[512,1024]{1,0:T(8,128)(2,1)}, bf16[512,1024]{1,0:T(8,128)(2,1)}, u32[]{:S(2)}, u32[]{:S(2)}) collective-permute-start(bf16[512,1024]{1,0:T(8,128)(2,1)} %add_convert_fusion.1), channel_id=1, source_target_pairs={{2,3},{3,2},{4,5},{5,4},{10,11},{11,10},{12,13},{13,12},{18,19},{1... | collective-permute-start | bytes 3145736 | tf_op jit(solution)/shard_map/ppermute | solution.py:992
  221.1 7.3 %copy-start.6 = (bf16[1024,1024]{1,0:T(8,128)(2,1)S(1)}, bf16[1024,1024]{1,0:T(8,128)(2,1)}, u32[]{:S(2)}) copy-start(bf16[1024,1024]{1,0:T(8,128)(2,1)} %get-tuple-element.170) | copy-start | bytes 6291460
  221.9 13.2 %collective-permute-start.19 = (bf16[320,768]{1,0:T(8,128)(2,1)}, bf16[320,768]{1,0:T(8,128)(2,1)S(1)}, u32[]{:S(2)}, u32[]{:S(2)}) collective-permute-start(bf16[320,768]{1,0:T(8,128)(2,1)} %get-tuple-element.209), channel_id=1, source_target_pairs={{0,8},{8,0},{16,24},{24,16},{1,9},{9,1},{17,25},{25,17},{2,10},{10... | collective-permute-start | bytes 1474568 | tf_op jit(solution)/shard_map/ppermute | solution.py:1034
  223.0 14.1 %collective-permute-start.20 = (bf16[320,768]{1,0:T(8,128)(2,1)}, bf16[320,768]{1,0:T(8,128)(2,1)S(1)}, u32[]{:S(2)}, u32[]{:S(2)}) collective-permute-start(bf16[320,768]{1,0:T(8,128)(2,1)} %get-tuple-element.210), channel_id=1, source_target_pairs={{0,16},{8,24},{16,0},{24,8},{1,17},{9,25},{17,1},{25,9},{2,18},{10... | collective-permute-start | bytes 1474568 | tf_op jit(solution)/shard_map/ppermute | solution.py:1034
  224.1 22.5 %collective-permute-start.21 = (bf16[320,768]{1,0:T(8,128)(2,1)}, bf16[320,768]{1,0:T(8,128)(2,1)S(1)}, u32[]{:S(2)}, u32[]{:S(2)}) collective-permute-start(bf16[320,768]{1,0:T(8,128)(2,1)} %get-tuple-element.211), channel_id=1, source_target_pairs={{0,24},{8,16},{16,8},{24,0},{1,25},{9,17},{17,9},{25,1},{2,26},{10... | collective-permute-start | bytes 1474568 | tf_op jit(solution)/shard_map/ppermute | solution.py:1034
  225.5 33.2 %collective-permute-start.22 = (bf16[320,1024]{1,0:T(8,128)(2,1)}, bf16[320,1024]{1,0:T(8,128)(2,1)S(1)}, u32[]{:S(2)}, u32[]{:S(2)}) collective-permute-start(bf16[320,1024]{1,0:T(8,128)(2,1)} %pad_maximum_fusion.1), channel_id=1, source_target_pairs={{0,2},{1,3},{2,0},{3,1},{4,6},{5,7},{6,4},{7,5},{8,10},{9,11},{10,... | collective-permute-start | bytes 1966088 | tf_op jit(solution)/shard_map/ppermute | solution.py:992
  231.9 14.9 %copy-start.22 = (bf16[256,768]{1,0:T(8,128)(2,1)S(1)}, bf16[256,768]{1,0:T(8,128)(2,1)}, u32[]{:S(2)}) copy-start(bf16[256,768]{1,0:T(8,128)(2,1)} %get-tuple-element.213) | copy-start | bytes 1179652
  251.4 7.5 %copy-start.11 = (f32[256,1024]{1,0:T(8,128)S(1)}, f32[256,1024]{1,0:T(8,128)}, u32[]{:S(2)}) copy-start(f32[256,1024]{1,0:T(8,128)} %copy-done.10) | copy-start | bytes 3145732
  251.4 28.9 %collective-permute-start.25 = (bf16[512,1024]{1,0:T(8,128)(2,1)S(1)}, bf16[512,1024]{1,0:T(8,128)(2,1)S(1)}, u32[]{:S(2)}, u32[]{:S(2)}) collective-permute-start(bf16[512,1024]{1,0:T(8,128)(2,1)S(1)} %fusion.13), channel_id=1, source_target_pairs={{0,1},{1,0},{6,7},{7,6},{2,4},{3,5},{4,2},{5,3},{8,9},{9,8},{14,15... | collective-permute-start | bytes 3145736 | tf_op jit(solution)/shard_map/ppermute | solution.py:992
  259.2 29.4 %collective-permute-start.23 = (bf16[128,1024]{1,0:T(8,128)(2,1)S(1)}, bf16[128,1024]{1,0:T(8,128)(2,1)S(1)}, u32[]{:S(2)}, u32[]{:S(2)}) collective-permute-start(bf16[128,1024]{1,0:T(8,128)(2,1)S(1)} %bitcast.122), channel_id=1, source_target_pairs={{0,1},{1,0},{2,3},{3,2},{4,5},{5,4},{6,7},{7,6},{8,9},{9,8},{10,11... | collective-permute-start | bytes 786440 | tf_op jit(solution)/shard_map/ppermute | solution.py:992
  263.0 25.5 %collective-permute-start.24 = (bf16[128,1024]{1,0:T(8,128)(2,1)S(1)}, bf16[128,1024]{1,0:T(8,128)(2,1)S(1)}, u32[]{:S(2)}, u32[]{:S(2)}) collective-permute-start(bf16[128,1024]{1,0:T(8,128)(2,1)S(1)} %get-tuple-element.243), channel_id=1, source_target_pairs={{0,0},{1,4},{2,6},{3,2},{4,1},{5,5},{6,7},{7,3},{8,8},{9,12},{10,1... | collective-permute-start | bytes 786440 | tf_op jit(solution)/shard_map/ppermute | solution.py:992
  263.7 31.7 %collective-permute-start.26 = (bf16[192,768]{1,0:T(8,128)(2,1)S(1)}, bf16[192,768]{1,0:T(8,128)(2,1)S(1)}, u32[]{:S(2)}, u32[]{:S(2)}) collective-permute-start(bf16[192,768]{1,0:T(8,128)(2,1)S(1)} %constant_dynamic-update-slice_fusion), channel_id=1, source_target_pairs={{0,2},{1,3},{2,0},{3,1},{4,6},{5,7},{6,4},{7,5},{8,10},{9,11},{10,... | collective-permute-start | bytes 884744 | tf_op jit(solution)/shard_map/ppermute | solution.py:992
  268.8 12.5 %copy-start.9 = (bf16[1,512,1024]{2,1,0:T(8,128)(2,1)S(1)}, bf16[1,512,1024]{2,1,0:T(8,128)(2,1)}, u32[]{:S(2)}) copy-start(bf16[1,512,1024]{2,1,0:T(8,128)(2,1)} %param.29) | copy-start | bytes 3145732
  288.5 8.1 %copy-start.20 = (bf16[128,1024]{1,0:T(8,128)(2,1)}, bf16[128,1024]{1,0:T(8,128)(2,1)S(1)}, u32[]{:S(2)}) copy-start(bf16[128,1024]{1,0:T(8,128)(2,1)S(1)} %collective-permute-done.23.got_ref) | copy-start | bytes 786436
  288.5 8.0 %copy-start.23 = (bf16[128,1024]{1,0:T(8,128)(2,1)}, bf16[128,1024]{1,0:T(8,128)(2,1)S(1)}, u32[]{:S(2)}) copy-start(bf16[128,1024]{1,0:T(8,128)(2,1)S(1)} %collective-permute-done.24.reduce_ref) | copy-start | bytes 786436
  288.6 8.0 %collective-permute-start.28 = (bf16[128,1024]{1,0:T(8,128)(2,1)S(1)}, bf16[128,1024]{1,0:T(8,128)(2,1)S(1)}, u32[]{:S(2)}, u32[]{:S(2)}) collective-permute-start(bf16[128,1024]{1,0:T(8,128)(2,1)S(1)} %pad_maximum_fusion.2), channel_id=1, source_target_pairs={{0,4},{1,5},{2,6},{3,7},{4,0},{5,1},{6,2},{7,3},{8,12},{9,13},{10,... | collective-permute-start | bytes 786440 | tf_op jit(solution)/shard_map/ppermute | solution.py:992
  295.5 7.1 %copy-start.13 = (bf16[128,768]{1,0:T(8,128)(2,1)}, bf16[128,768]{1,0:T(8,128)(2,1)S(1)}, u32[]{:S(2)}) copy-start(bf16[128,768]{1,0:T(8,128)(2,1)S(1)} %fusion.19) | copy-start | bytes 589828
  295.7 6.9 %collective-permute-start.27 = (bf16[128,768]{1,0:T(8,128)(2,1)S(1)}, bf16[128,768]{1,0:T(8,128)(2,1)S(1)}, u32[]{:S(2)}, u32[]{:S(2)}) collective-permute-start(bf16[128,768]{1,0:T(8,128)(2,1)S(1)} %constant_dynamic-update-slice_fusion.5), channel_id=1, source_target_pairs={{0,1},{1,0},{2,3},{3,2},{4,5},{5,4},{6,7},{7,6},{8,9},{9,8},{10,11... | collective-permute-start | bytes 589832 | tf_op jit(solution)/shard_map/ppermute | solution.py:992
  302.7 1.5 collective-permute-start.29
  (13 other events, 25.3 us)
